TPU v7x, 512 devices: a whole 4x8x8 slice. The times are simulated.
512 devices in a mesh: space: 64 (over y, x, core), tm: 8 (over z).
Axes of the slice: x: 4, y: 8, z: 8, core: 2. Of those that a mesh axis runs over, the one named last changes fastest.
Arguments:
- dipole_rates: bfloat16 [4096, 3, 8192], P('space', None, 'tm'), may hold values from -6 to 6
- polar_rates: bfloat16 [4096, 3, 8192], P('space', None, 'tm'), may hold values from -6 to 6
- pair_counts: int32 [64, 64], P('space'), may hold values from 0 to 24, as said below
- send_blocks: int32 [64, 64, 24], P('space'), may hold values from 0 to 31, as said below
- partners: int32 [2048, 24], P('space'), may hold values from 0 to 176, as said below
Outputs:
- correlations: float32 [64, 4, 1024], P('space', None, 'tm')
Inputs may be any that keep to these rules, and one draw needn't show every extreme that they name: pair_counts[e, d] is 0 unless d differs from e by 1 to 3 domains cyclically; for every sending domain e exactly one receiving domain has 24. The entries of send_blocks[e, d] are distinct block numbers of domain e; entries at or past pair_counts[e, d] are stale. `partners`: the entries of one block's list are distinct except for the empty entry 176; an entry below 32 is never the block itself.
All inputs are finite; a program needn't handle non-finite values.
Results may differ from a plain program's by a relative error of at most 0.0052.
Values may be sent and summed in bfloat16 or wider, within the bound.
No kernel may reach another device: no remote copies, remote signals or barrier semaphores. Data moves between devices by JAX's collectives and lax.ppermute only.
A program may use at most 128 MiB of HBM per device.

v0:
```python
import jax
import jax.numpy as jnp
from jax import lax
from jax.experimental import pallas as pl
from jax.experimental.pallas import tpu as pltpu
from jax.sharding import PartitionSpec as P

BLK = 2
LAGS = 1024
REACH = 3
LANE = 128
TILE = 256
VMEM_BYTES = 32 * 1024 * 1024


def pair_sums(rates):
    molecules = rates.shape[0]
    row = lax.broadcasted_iota(jnp.int32, (molecules // BLK, molecules), 0)
    col = lax.broadcasted_iota(jnp.int32, (molecules // BLK, molecules), 1)
    ones = ((col >= row * BLK) & (col < row * BLK + BLK)).astype(jnp.bfloat16)
    return jnp.dot(ones, rates, preferred_element_type=jnp.float32).astype(jnp.bfloat16)


def pack_kernel(domain_ref, dipole_ref, counts_ref, lists_ref, pack_ref):
    components, molecules, length = dipole_ref.shape
    blocks = molecules // BLK
    rows = components * blocks
    for c in range(components):
        totals = pair_sums(dipole_ref[c])
        for j in range(length // LANE):
            at = j * rows + c * blocks
            pack_ref[at : at + blocks, :] = totals[:, j * LANE : (j + 1) * LANE]
    capacity, domains = lists_ref.shape
    slot = lax.broadcasted_iota(jnp.int32, (16, domains), 0)
    offset = jnp.where(slot < REACH, slot - REACH, slot - REACH + 1)
    target = lax.rem(domain_ref[0] + offset + domains, domains)
    hot = (lax.broadcasted_iota(jnp.int32, (16, domains), 1) == target) & (slot < 2 * REACH)
    picked = lax.dot_general(
        hot.astype(jnp.bfloat16),
        lists_ref[...].astype(jnp.float32).astype(jnp.bfloat16),
        (((1,), (1,)), ((), ())),
        preferred_element_type=jnp.float32,
    )
    count = jnp.sum(jnp.where(hot, counts_ref[...], 0).astype(jnp.float32), axis=1, keepdims=True)
    entry = lax.broadcasted_iota(jnp.int32, (16, capacity), 1).astype(jnp.float32)
    meta = jnp.where(entry < count, picked, -1.0)
    meta = jnp.concatenate([meta, jnp.full((16, LANE - capacity), -1.0, jnp.float32)], axis=1)
    base = rows * (length // LANE)
    pack_ref[base : base + 16, :] = meta.astype(jnp.bfloat16)


def own_kernel(pack_ref, polar_ref, own_ref):
    components, molecules, length = polar_ref.shape
    blocks = molecules // BLK
    rows = components * blocks
    for j in range(length // LANE):
        own_ref[0:rows, j * LANE : (j + 1) * LANE] = pack_ref[j * rows : (j + 1) * rows, :]
    for c in range(components):
        own_ref[rows + c * blocks : rows + (c + 1) * blocks, :] = pair_sums(polar_ref[c])


def fold(gram):
    width = gram.shape[1]
    height = gram.shape[0]
    while height > LANE:
        height //= 2
        width -= height
        gram = gram[:height, :width] + gram[height:, height : height + width]
    while height > 8:
        height //= 2
        gram = gram[:height] + pltpu.roll(gram[height:], width - height, 1)
    row = lax.broadcasted_iota(jnp.int32, gram.shape, 0)
    for bit in (4, 2, 1):
        gram = jnp.where((row & bit) != 0, pltpu.roll(gram, width - bit, 1), gram)
    return jnp.sum(gram, axis=0, keepdims=True)


def sums_kernel(
    odd_ref, partners_ref, pack_ref, pa_ref, pb_ref, far_ref, spa_ref, spb_ref, sown_ref, own_ref, next_ref, out_ref, field_ref
):
    slots, blocks = partners_ref.shape
    rows = 3 * blocks
    length = own_ref.shape[1]
    odd = odd_ref[0] == 1
    capacity = slots
    received = (
        (pa_ref, 4, 1),
        (pb_ref, 1, 4),
        (far_ref, 0, 5),
        (spa_ref, 2, 3),
        (spb_ref, 5, 0),
        (sown_ref, 3, 2),
    )

    entry = lax.broadcasted_iota(jnp.int32, (blocks, blocks), 0)

    def chosen(first):
        total = jnp.zeros((blocks, blocks), jnp.float32)
        wanted = entry + first
        for s in range(slots):
            total = total + jnp.where(partners_ref[s : s + 1, :] == wanted, 1.0, 0.0)
        return total

    weights = [chosen(0).astype(jnp.bfloat16)]
    base = rows * (length // LANE)
    slot_row = lax.broadcasted_iota(jnp.int32, (16, LANE), 0)
    number = lax.broadcasted_iota(jnp.int32, (blocks, blocks), 0).astype(jnp.float32)
    for ref, at_even, at_odd in received:
        place = jnp.where(odd, at_odd, at_even)
        meta = ref[base : base + 16, :].astype(jnp.float32)
        listed = jnp.sum(jnp.where(slot_row == 2 * REACH - 1 - place, meta, 0.0), axis=0, keepdims=True)
        select = (listed[:, :blocks] == number).astype(jnp.bfloat16)
        wanted = chosen(blocks + place * capacity).astype(jnp.bfloat16)
        weights.append(jnp.dot(select, wanted, preferred_element_type=jnp.float32).astype(jnp.bfloat16))
    weight = jnp.concatenate(weights, axis=0)
    sources = [pack_ref] + [r[0] for r in received]

    for c in range(3):
        for j in range(0, length // LANE, 2):
            parts = []
            for jj in (j, j + 1):
                at = jj * rows + c * blocks
                parts.append(jnp.concatenate([ref[at : at + blocks, :] for ref in sources], axis=0))
            table = jnp.concatenate(parts, axis=1)
            field = lax.dot_general(
                weight, table, (((0,), (0,)), ((), ())), preferred_element_type=jnp.float32
            )
            field_ref[c * blocks : (c + 1) * blocks, j * LANE : (j + 2) * LANE] = field.astype(jnp.bfloat16)

    span = TILE + LAGS
    steps = length // TILE

    def later(first, count, i):
        lo = i * TILE
        here = own_ref[first : first + count, lo:length]
        return jnp.concatenate([here, next_ref[first : first + count, 0 : span - (length - lo)]], axis=1)

    def gram(anchor_first, window_first, count):
        anchors = jnp.concatenate(
            [field_ref[anchor_first : anchor_first + count, i * TILE : (i + 1) * TILE] for i in range(steps)], axis=0
        )
        window = jnp.concatenate([later(window_first, count, i) for i in range(steps)], axis=0)
        return lax.dot_general(anchors, window, (((0,), (0,)), ((), ())), preferred_element_type=jnp.float32)

    for q in range(4):
        if q == 0:
            sums = fold(gram(0, 0, rows))
        else:
            sums = fold(gram(2 * blocks, rows + (q - 1) * blocks, blocks))
        for j in range(LAGS // LANE):
            out_ref[j, q : q + 1, :] = sums[:, j * LANE : (j + 1) * LANE]


VMEM = pl.BlockSpec(memory_space=pltpu.VMEM)
SMEM = pl.BlockSpec(memory_space=pltpu.SMEM)
PARAMS = pltpu.CompilerParams(vmem_limit_bytes=VMEM_BYTES)


def per_device(dipole_rates, polar_rates, pair_counts, send_blocks, partners):
    space_size = lax.axis_size("space")
    time_size = lax.axis_size("tm")
    domain = lax.axis_index("space").astype(jnp.int32)
    molecules, components, length = dipole_rates.shape
    blocks = molecules // BLK
    rows = components * blocks
    pack_rows = rows * (length // LANE) + 16
    bf16 = jnp.bfloat16

    def moved(value, by_even, by_odd):
        pairs = [(i, (i + (by_odd if i % 2 else by_even)) % space_size) for i in range(space_size)]
        return lax.ppermute(value, "space", pairs)

    pack = pl.pallas_call(
        pack_kernel,
        out_shape=jax.ShapeDtypeStruct((pack_rows, LANE), bf16),
        in_specs=[SMEM, VMEM, VMEM, VMEM],
        out_specs=VMEM,
        compiler_params=PARAMS,
        cost_estimate=pl.CostEstimate(flops=2 * 32 * 64 * 3072, bytes_accessed=600000, transcendentals=0),
        name="pack",
    )(domain[None], dipole_rates.transpose(1, 0, 2), pair_counts, send_blocks[0].T)
    own = pl.pallas_call(
        own_kernel,
        out_shape=jax.ShapeDtypeStruct((2 * rows, length), bf16),
        in_specs=[VMEM, VMEM],
        out_specs=VMEM,
        compiler_params=PARAMS,
        cost_estimate=pl.CostEstimate(flops=2 * 32 * 64 * 3072, bytes_accessed=980000, transcendentals=0),
        name="own",
    )(pack, polar_rates.transpose(1, 0, 2))

    pa = moved(pack, -2, 2)
    pb = moved(pack, 2, -2)
    following = lax.ppermute(own, "tm", [(i, i - 1) for i in range(1, time_size)])
    sown = moved(pack, 1, -1)
    far = moved(pa, -1, 1)
    spa = moved(pa, 1, -1)
    spb = moved(pb, 1, -1)

    sums = pl.pallas_call(
        sums_kernel,
        out_shape=jax.ShapeDtypeStruct((LAGS // LANE, 4, LANE), jnp.float32),
        in_specs=[SMEM] + [VMEM] * 10,
        out_specs=VMEM,
        scratch_shapes=[pltpu.VMEM((rows, length), bf16)],
        compiler_params=PARAMS,
        cost_estimate=pl.CostEstimate(flops=2 * 300000000, bytes_accessed=2500000, transcendentals=0),
        name="sums",
    )((domain % 2)[None], partners.T, pack, pa, pb, far, spa, spb, sown, own, following)

    shares = lax.all_to_all(sums, "tm", 0, 0)
    lag_share = LAGS // time_size
    lag_index = lax.axis_index("tm") * lag_share + jnp.arange(lag_share, dtype=jnp.int32)
    anchor_count = (length * time_size - lag_index).astype(jnp.float32)
    return (jnp.sum(shares, axis=0) / anchor_count[None, :])[None]


def solution(mesh):
    return jax.shard_map(
        per_device,
        mesh=mesh,
        in_specs=(
            P("space", None, "tm"),
            P("space", None, "tm"),
            P("space", None),
            P("space", None, None),
            P("space", None),
        ),
        out_specs=P("space", None, "tm"),
        check_vma=False,
    )
```

profile of v0, /device:TPU:32, one launch (start us, length us, event | category | flops | bytes accessed | tf_op | source)
XLA Modules:
  0.0 52.0 jit_solution(2729696918123761395)
XLA Ops:
  0.0 0.0 copy-start.3
  0.0 0.0 copy-start.4
  0.0 0.7 %copy-done.3 = s32[1,64,24]{1,2,0:T(8,128)S(1)} copy-done((s32[1,64,24]{1,2,0:T(8,128)S(1)}, s32[1,64,24]{1,2,0:T(8,128)}, u32[]{:S(2)}) %copy-start.3) | copy-done | bytes 6168
  0.7 0.0 copy-done.4
  0.7 0.0 copy-start
  0.7 1.0 %copy-done = bf16[64,3,1024]{2,0,1:T(8,128)(2,1)S(1)} copy-done((bf16[64,3,1024]{2,0,1:T(8,128)(2,1)S(1)}, bf16[64,3,1024]{2,0,1:T(8,128)(2,1)}, u32[]{:S(2)}) %copy-start) | copy-done | bytes 393240
  1.7 0.0 copy-start.1
  1.7 0.2 pack.1.pack_ref
  1.9 3.4 %collective-permute-start.1 = (bf16[784,128]{1,0:T(8,128)(2,1)S(1)}, bf16[784,128]{1,0:T(8,128)(2,1)S(1)}, u32[]{:S(2)}, u32[]{:S(2)}) collective-permute-start(bf16[784,128]{1,0:T(8,128)(2,1)S(1)} %pack.1.pack_ref), channel_id=1, source_target_pairs={{0,16},{8,504},{16,32},{24,8},{32,48},{40,24},{48,64},{56,40},{64,... | collective-permute-start | bytes 602120 | tf_op jit(solution)/shard_map/ppermute | solution.py:171
  5.3 5.8 %collective-permute-start = (bf16[784,128]{1,0:T(8,128)(2,1)S(1)}, bf16[784,128]{1,0:T(8,128)(2,1)S(1)}, u32[]{:S(2)}, u32[]{:S(2)}) collective-permute-start(bf16[784,128]{1,0:T(8,128)(2,1)S(1)} %pack.1.pack_ref), channel_id=1, source_target_pairs={{0,496},{8,24},{16,0},{24,40},{32,16},{40,56},{48,32},{56,72},{64,... | collective-permute-start | bytes 602120 | tf_op jit(solution)/shard_map/ppermute | solution.py:171
  11.1 0.0 copy-done.1
  11.1 0.2 own.1.own_ref
  11.3 1.3 %collective-permute-start.6 = (bf16[192,1024]{1,0:T(8,128)(2,1)S(1)}, bf16[192,1024]{1,0:T(8,128)(2,1)S(1)}, u32[]{:S(2)}, u32[]{:S(2)}) collective-permute-start(bf16[192,1024]{1,0:T(8,128)(2,1)S(1)} %own.1.own_ref), channel_id=1, source_target_pairs={{1,0},{2,1},{3,2},{4,3},{5,4},{6,5},{7,6},{9,8},{10,9},{11,10},{12... | collective-permute-start | bytes 1179656 | tf_op jit(solution)/shard_map/ppermute | solution.py:194
  12.6 1.9 %collective-permute-start.5 = (bf16[784,128]{1,0:T(8,128)(2,1)S(1)}, bf16[784,128]{1,0:T(8,128)(2,1)S(1)}, u32[]{:S(2)}, u32[]{:S(2)}) collective-permute-start(bf16[784,128]{1,0:T(8,128)(2,1)S(1)} %pack.1.pack_ref), channel_id=1, source_target_pairs={{0,8},{8,0},{16,24},{24,16},{32,40},{40,32},{48,56},{56,48},{64,72... | collective-permute-start | bytes 602120 | tf_op jit(solution)/shard_map/ppermute | solution.py:171
  14.5 0.0 collective-permute-done.1.pb_ref
  14.5 2.4 %collective-permute-start.4 = (bf16[784,128]{1,0:T(8,128)(2,1)S(1)}, bf16[784,128]{1,0:T(8,128)(2,1)S(1)}, u32[]{:S(2)}, u32[]{:S(2)}) collective-permute-start(bf16[784,128]{1,0:T(8,128)(2,1)S(1)} %collective-permute-done.1.pb_ref), channel_id=1, source_target_pairs={{0,8},{8,0},{16,24},{24,16},{32,40},{40,32},{48,56},{56,48},{64,72... | collective-permute-start | bytes 602120 | tf_op jit(solution)/shard_map/ppermute | solution.py:171
  16.9 0.0 collective-permute-done.pa_ref
  17.0 1.9 %collective-permute-start.3 = (bf16[784,128]{1,0:T(8,128)(2,1)S(1)}, bf16[784,128]{1,0:T(8,128)(2,1)S(1)}, u32[]{:S(2)}, u32[]{:S(2)}) collective-permute-start(bf16[784,128]{1,0:T(8,128)(2,1)S(1)} %collective-permute-done.pa_ref), channel_id=1, source_target_pairs={{0,8},{8,0},{16,24},{24,16},{32,40},{40,32},{48,56},{56,48},{64,72... | collective-permute-start | bytes 602120 | tf_op jit(solution)/shard_map/ppermute | solution.py:171
  18.9 5.1 %collective-permute-start.2 = (bf16[784,128]{1,0:T(8,128)(2,1)S(1)}, bf16[784,128]{1,0:T(8,128)(2,1)S(1)}, u32[]{:S(2)}, u32[]{:S(2)}) collective-permute-start(bf16[784,128]{1,0:T(8,128)(2,1)S(1)} %collective-permute-done.pa_ref), channel_id=1, source_target_pairs={{0,504},{8,16},{16,8},{24,32},{32,24},{40,48},{48,40},{56,64},{64,... | collective-permute-start | bytes 602120 | tf_op jit(solution)/shard_map/ppermute | solution.py:171
  24.0 0.0 copy-start.2
  24.1 0.0 collective-permute-done.5.sown_ref
  24.1 0.0 collective-permute-done.6.next_ref
  24.1 0.0 collective-permute-done.4.spb_ref
  24.1 0.0 collective-permute-done.3.spa_ref
  24.1 5.1 %collective-permute-done.2.far_ref = bf16[784,128]{1,0:T(8,128)(2,1)S(1)} collective-permute-done((bf16[784,128]{1,0:T(8,128)(2,1)S(1)}, bf16[784,128]{1,0:T(8,128)(2,1)S(1)}, u32[]{:S(2)}, u32[]{:S(2)}) %collective-permute-start.2) | collective-permute-done | bytes 200736 | tf_op jit(solution)/shard_map/ppermute | solution.py:171
  29.2 0.0 copy-done.2
  29.2 2.9 %sums.1 = f32[8,4,128]{2,1,0:T(4,128)} custom-call(s32[1]{0:T(128)} %bitcast.odd_ref, s32[24,32]{1,0:T(8,128)S(1)} %bitcast.12, bf16[784,128]{1,0:T(8,128)(2,1)S(1)} %pack.1.pack_ref, bf16[784,128]{1,0:T(8,128)(2,1)S(1)} %collective-permute-done.pa_ref, bf16[784,128]{1,0:T(8,128)(2,1)S(1)} %collective-permute-done.1.pb_ref, ...), custom_call_target="tpu_custom_call" | custom-call | flops 600000000 | bytes 2500000 | tf_op jit(solution)/shard_map/sums/pallas_call | solution.py:200
  32.2 11.5 %all-to-all-start = ((f32[8,4,128]{2,1,0:T(4,128)}), f32[8,4,128]{2,1,0:T(4,128)S(1)}, u32[]{:S(2)}, u32[]{:S(2)}) async-start(f32[8,4,128]{2,1,0:T(4,128)} %sums.1), calls=%async_computation | async-start | bytes 32768 | tf_op jit(solution)/shard_map/all_to_all | solution.py:211
  43.7 7.8 %all-to-all-done = f32[8,4,128]{2,1,0:T(4,128)S(1)} async-done(((f32[8,4,128]{2,1,0:T(4,128)}), f32[8,4,128]{2,1,0:T(4,128)S(1)}, u32[]{:S(2)}, u32[]{:S(2)}) %all-to-all-start) | async-done | bytes 16416 | tf_op jit(solution)/shard_map/all_to_all | solution.py:211
  51.5 0.6 %bitcast_divide_fusion = f32[1,4,128]{2,1,0:T(4,128)} fusion(f32[4,128]{1,0:T(4,128)S(1)} %reduce_sum.11, f32[128]{0:T(128)S(1)} %subtract_convert_fusion), kind=kLoop, calls=%fused_computation | loop fusion | flops 512 | bytes 4608 | tf_op jit(solution)/shard_map/div | solution.py:215
  (2 shorter events, 0.0 us)
Async XLA Ops:
  0.0 0.7 %copy-start.3 = (s32[1,64,24]{1,2,0:T(8,128)S(1)}, s32[1,64,24]{1,2,0:T(8,128)}, u32[]{:S(2)}) copy-start(s32[1,64,24]{1,2,0:T(8,128)} %param.8) | copy-start | bytes 18436
  0.0 0.7 %copy-start.4 = (s32[1,64]{1,0:T(1,128)S(1)}, s32[1,64]{1,0:T(1,128)}, u32[]{:S(2)}) copy-start(s32[1,64]{1,0:T(1,128)} %counts_ref.1) | copy-start | bytes 772
  0.7 1.0 %copy-start = (bf16[64,3,1024]{2,0,1:T(8,128)(2,1)S(1)}, bf16[64,3,1024]{2,0,1:T(8,128)(2,1)}, u32[]{:S(2)}) copy-start(bf16[64,3,1024]{2,0,1:T(8,128)(2,1)} %param.5) | copy-start | bytes 1179652
  1.7 9.4 %copy-start.1 = (bf16[64,3,1024]{2,0,1:T(8,128)(2,1)S(1)}, bf16[64,3,1024]{2,0,1:T(8,128)(2,1)}, u32[]{:S(2)}) copy-start(bf16[64,3,1024]{2,0,1:T(8,128)(2,1)} %param.6) | copy-start | bytes 1179652
  1.9 12.6 %collective-permute-start.1 = (bf16[784,128]{1,0:T(8,128)(2,1)S(1)}, bf16[784,128]{1,0:T(8,128)(2,1)S(1)}, u32[]{:S(2)}, u32[]{:S(2)}) collective-permute-start(bf16[784,128]{1,0:T(8,128)(2,1)S(1)} %pack.1.pack_ref), channel_id=1, source_target_pairs={{0,16},{8,504},{16,32},{24,8},{32,48},{40,24},{48,64},{56,40},{64,... | collective-permute-start | bytes 602120 | tf_op jit(solution)/shard_map/ppermute | solution.py:171
  5.3 11.6 %collective-permute-start = (bf16[784,128]{1,0:T(8,128)(2,1)S(1)}, bf16[784,128]{1,0:T(8,128)(2,1)S(1)}, u32[]{:S(2)}, u32[]{:S(2)}) collective-permute-start(bf16[784,128]{1,0:T(8,128)(2,1)S(1)} %pack.1.pack_ref), channel_id=1, source_target_pairs={{0,496},{8,24},{16,0},{24,40},{32,16},{40,56},{48,32},{56,72},{64,... | collective-permute-start | bytes 602120 | tf_op jit(solution)/shard_map/ppermute | solution.py:171
  11.3 12.8 %collective-permute-start.6 = (bf16[192,1024]{1,0:T(8,128)(2,1)S(1)}, bf16[192,1024]{1,0:T(8,128)(2,1)S(1)}, u32[]{:S(2)}, u32[]{:S(2)}) collective-permute-start(bf16[192,1024]{1,0:T(8,128)(2,1)S(1)} %own.1.own_ref), channel_id=1, source_target_pairs={{1,0},{2,1},{3,2},{4,3},{5,4},{6,5},{7,6},{9,8},{10,9},{11,10},{12... | collective-permute-start | bytes 1179656 | tf_op jit(solution)/shard_map/ppermute | solution.py:194
  12.6 11.5 %collective-permute-start.5 = (bf16[784,128]{1,0:T(8,128)(2,1)S(1)}, bf16[784,128]{1,0:T(8,128)(2,1)S(1)}, u32[]{:S(2)}, u32[]{:S(2)}) collective-permute-start(bf16[784,128]{1,0:T(8,128)(2,1)S(1)} %pack.1.pack_ref), channel_id=1, source_target_pairs={{0,8},{8,0},{16,24},{24,16},{32,40},{40,32},{48,56},{56,48},{64,72... | collective-permute-start | bytes 602120 | tf_op jit(solution)/shard_map/ppermute | solution.py:171
  14.5 9.6 %collective-permute-start.4 = (bf16[784,128]{1,0:T(8,128)(2,1)S(1)}, bf16[784,128]{1,0:T(8,128)(2,1)S(1)}, u32[]{:S(2)}, u32[]{:S(2)}) collective-permute-start(bf16[784,128]{1,0:T(8,128)(2,1)S(1)} %collective-permute-done.1.pb_ref), channel_id=1, source_target_pairs={{0,8},{8,0},{16,24},{24,16},{32,40},{40,32},{48,56},{56,48},{64,72... | collective-permute-start | bytes 602120 | tf_op jit(solution)/shard_map/ppermute | solution.py:171
  17.0 7.1 %collective-permute-start.3 = (bf16[784,128]{1,0:T(8,128)(2,1)S(1)}, bf16[784,128]{1,0:T(8,128)(2,1)S(1)}, u32[]{:S(2)}, u32[]{:S(2)}) collective-permute-start(bf16[784,128]{1,0:T(8,128)(2,1)S(1)} %collective-permute-done.pa_ref), channel_id=1, source_target_pairs={{0,8},{8,0},{16,24},{24,16},{32,40},{40,32},{48,56},{56,48},{64,72... | collective-permute-start | bytes 602120 | tf_op jit(solution)/shard_map/ppermute | solution.py:171
  18.9 10.4 %collective-permute-start.2 = (bf16[784,128]{1,0:T(8,128)(2,1)S(1)}, bf16[784,128]{1,0:T(8,128)(2,1)S(1)}, u32[]{:S(2)}, u32[]{:S(2)}) collective-permute-start(bf16[784,128]{1,0:T(8,128)(2,1)S(1)} %collective-permute-done.pa_ref), channel_id=1, source_target_pairs={{0,504},{8,16},{16,8},{24,32},{32,24},{40,48},{48,40},{56,64},{64,... | collective-permute-start | bytes 602120 | tf_op jit(solution)/shard_map/ppermute | solution.py:171
  24.0 5.2 %copy-start.2 = (s32[32,24]{0,1:T(8,128)S(1)}, s32[32,24]{0,1:T(8,128)}, u32[]{:S(2)}) copy-start(s32[32,24]{0,1:T(8,128)} %param.9) | copy-start | bytes 9220
  32.2 19.3 %all-to-all-start = ((f32[8,4,128]{2,1,0:T(4,128)}), f32[8,4,128]{2,1,0:T(4,128)S(1)}, u32[]{:S(2)}, u32[]{:S(2)}) async-start(f32[8,4,128]{2,1,0:T(4,128)} %sums.1), calls=%async_computation | async-start | bytes 32768 | tf_op jit(solution)/shard_map/all_to_all | solution.py:211
where the time goes:
time: 52.5 us; the launch traced here: 52 us
  starting transfers between devices  33.3 us (63%)
  waiting for transfers between devices  12.9 us (25%)
  Pallas kernels  3.3 us (6%)
  local copies, waits for them, and re-layouts  1.71 us (3%)
  other arithmetic  0.61 us (1%)
    ppermute x6, starting transfers between devices, moved(): return lax.ppermute(value, 'space', pairs)  20.6 us
    all_to_all x1, starting transfers between devices, per_device(): shares = lax.all_to_all(sums, 'tm', 0, 0)  11.5 us
    all_to_all x1, waiting for transfers between devices, per_device(): shares = lax.all_to_all(sums, 'tm', 0, 0)  7.77 us
    ppermute x6, waiting for transfers between devices, moved(): return lax.ppermute(value, 'space', pairs)  5.15 us
    pallas_call x1, Pallas kernels, per_device(): pl.pallas_call(sums_kernel, out_shape=jax.ShapeDtypeStruct((LAGS // LANE,...  2.91 us
    unnamed x10, local copies, waits for them, and re-layouts  1.71 us
    ppermute x1, starting transfers between devices, per_device(): lax.ppermute(own, 'tm', [(i, i - 1) for i in range(1, time_size)])  1.29 us
  transfers between devices with their start and end apart: 8, of which 2 were waited for; matrix products, arithmetic and copies ran while one was open for 0% of the time, Pallas kernels for 0%

commit v1 on v0

--- a/solution.py
+++ b/solution.py
@@ -9,7 +9,7 @@
 LAGS = 1024
 REACH = 3
 LANE = 128
-TILE = 256
+TILE = 128
 VMEM_BYTES = 32 * 1024 * 1024
 
 
@@ -21,15 +21,26 @@
     return jnp.dot(ones, rates, preferred_element_type=jnp.float32).astype(jnp.bfloat16)
 
 
-def pack_kernel(domain_ref, dipole_ref, counts_ref, lists_ref, pack_ref):
+def totals_kernel(dipole_hbm, polar_hbm, own_ref, dipole_ref, polar_ref, sem):
     components, molecules, length = dipole_ref.shape
     blocks = molecules // BLK
-    rows = components * blocks
-    for c in range(components):
-        totals = pair_sums(dipole_ref[c])
-        for j in range(length // LANE):
-            at = j * rows + c * blocks
-            pack_ref[at : at + blocks, :] = totals[:, j * LANE : (j + 1) * LANE]
+    copies = [
+        pltpu.make_async_copy(dipole_hbm, dipole_ref, sem.at[0]),
+        pltpu.make_async_copy(polar_hbm, polar_ref, sem.at[1]),
+    ]
+    for copy in copies:
+        copy.start()
+    for number, (copy, ref) in enumerate(zip(copies, (dipole_ref, polar_ref))):
+        copy.wait()
+        for c in range(components):
+            at = (number * components + c) * blocks
+            own_ref[at : at + blocks, :] = pair_sums(ref[c])
+
+
+def pack_kernel(domain_ref, own_ref, counts_ref, lists_ref, pack_ref):
+    rows, length = own_ref.shape
+    for j in range(length // LANE):
+        pack_ref[j * rows : (j + 1) * rows, :] = own_ref[:, j * LANE : (j + 1) * LANE]
     capacity, domains = lists_ref.shape
     slot = lax.broadcasted_iota(jnp.int32, (16, domains), 0)
     offset = jnp.where(slot < REACH, slot - REACH, slot - REACH + 1)
@@ -49,14 +60,10 @@
     pack_ref[base : base + 16, :] = meta.astype(jnp.bfloat16)
 
 
-def own_kernel(pack_ref, polar_ref, own_ref):
-    components, molecules, length = polar_ref.shape
-    blocks = molecules // BLK
-    rows = components * blocks
-    for j in range(length // LANE):
-        own_ref[0:rows, j * LANE : (j + 1) * LANE] = pack_ref[j * rows : (j + 1) * rows, :]
-    for c in range(components):
-        own_ref[rows + c * blocks : rows + (c + 1) * blocks, :] = pair_sums(polar_ref[c])
+def join_kernel(first_ref, second_ref, third_ref, joined_ref):
+    count = first_ref.shape[0]
+    for i, ref in enumerate((first_ref, second_ref, third_ref)):
+        joined_ref[i * count : (i + 1) * count, :] = ref[...]
 
 
 def fold(gram):
@@ -75,46 +82,28 @@
     return jnp.sum(gram, axis=0, keepdims=True)
 
 
-def sums_kernel(
-    odd_ref, partners_ref, pack_ref, pa_ref, pb_ref, far_ref, spa_ref, spb_ref, sown_ref, own_ref, next_ref, out_ref, field_ref
-):
-    slots, blocks = partners_ref.shape
-    rows = 3 * blocks
-    length = own_ref.shape[1]
-    odd = odd_ref[0] == 1
-    capacity = slots
-    received = (
-        (pa_ref, 4, 1),
-        (pb_ref, 1, 4),
-        (far_ref, 0, 5),
-        (spa_ref, 2, 3),
-        (spb_ref, 5, 0),
-        (sown_ref, 3, 2),
-    )
-
-    entry = lax.broadcasted_iota(jnp.int32, (blocks, blocks), 0)
-
-    def chosen(first):
-        total = jnp.zeros((blocks, blocks), jnp.float32)
-        wanted = entry + first
-        for s in range(slots):
-            total = total + jnp.where(partners_ref[s : s + 1, :] == wanted, 1.0, 0.0)
-        return total
-
-    weights = [chosen(0).astype(jnp.bfloat16)]
-    base = rows * (length // LANE)
+def weights_of(place, meta_ref, partners_ref):
+    slots, blocks = partners_ref.shape
     slot_row = lax.broadcasted_iota(jnp.int32, (16, LANE), 0)
     number = lax.broadcasted_iota(jnp.int32, (blocks, blocks), 0).astype(jnp.float32)
-    for ref, at_even, at_odd in received:
-        place = jnp.where(odd, at_odd, at_even)
-        meta = ref[base : base + 16, :].astype(jnp.float32)
-        listed = jnp.sum(jnp.where(slot_row == 2 * REACH - 1 - place, meta, 0.0), axis=0, keepdims=True)
-        select = (listed[:, :blocks] == number).astype(jnp.bfloat16)
-        wanted = chosen(blocks + place * capacity).astype(jnp.bfloat16)
-        weights.append(jnp.dot(select, wanted, preferred_element_type=jnp.float32).astype(jnp.bfloat16))
-    weight = jnp.concatenate(weights, axis=0)
-    sources = [pack_ref] + [r[0] for r in received]
-
+    meta = meta_ref[...].astype(jnp.float32)
+    listed = jnp.sum(jnp.where(slot_row == 2 * REACH - 1 - place, meta, 0.0), axis=0, keepdims=True)
+    select = (listed[:, :blocks] == number).astype(jnp.bfloat16)
+    wanted = named_by(blocks + place * slots, partners_ref).astype(jnp.bfloat16)
+    return jnp.dot(select, wanted, preferred_element_type=jnp.float32).astype(jnp.bfloat16)
+
+
+def named_by(first, partners_ref):
+    slots, blocks = partners_ref.shape
+    wanted = lax.broadcasted_iota(jnp.int32, (blocks, blocks), 0) + first
+    total = jnp.zeros((blocks, blocks), jnp.float32)
+    for s in range(slots):
+        total = total + jnp.where(partners_ref[s : s + 1, :] == wanted, 1.0, 0.0)
+    return total
+
+
+def field_terms(weight, sources, blocks, length, store):
+    rows = 3 * blocks
     for c in range(3):
         for j in range(0, length // LANE, 2):
             parts = []
@@ -125,7 +114,40 @@
             field = lax.dot_general(
                 weight, table, (((0,), (0,)), ((), ())), preferred_element_type=jnp.float32
             )
-            field_ref[c * blocks : (c + 1) * blocks, j * LANE : (j + 2) * LANE] = field.astype(jnp.bfloat16)
+            store(slice(c * blocks, (c + 1) * blocks), slice(j * LANE, (j + 2) * LANE), field)
+
+
+def near_kernel(odd_ref, partners_ref, pack_ref, pa_ref, pb_ref, part_ref):
+    slots, blocks = partners_ref.shape
+    rows, length = part_ref.shape
+    base = rows * (length // LANE)
+    odd = odd_ref[0] == 1
+    weights = [named_by(0, partners_ref).astype(jnp.bfloat16)]
+    for ref, at_even, at_odd in ((pa_ref, 4, 1), (pb_ref, 1, 4)):
+        weights.append(weights_of(jnp.where(odd, at_odd, at_even), ref.at[pl.ds(base, 16)], partners_ref))
+
+    def store(row, col, field):
+        part_ref[row, col] = field
+
+    field_terms(jnp.concatenate(weights, axis=0), [pack_ref, pa_ref, pb_ref], blocks, length, store)
+
+
+def sums_kernel(odd_ref, partners_ref, part_ref, far_ref, swap_ref, own_ref, next_ref, out_ref, field_ref):
+    slots, blocks = partners_ref.shape
+    rows = 3 * blocks
+    length = own_ref.shape[1]
+    base = rows * (length // LANE)
+    odd = odd_ref[0] == 1
+    count = far_ref.shape[0]
+    sown_ref, spa_ref, spb_ref = [swap_ref.at[pl.ds(i * count, count)] for i in range(3)]
+    weights = []
+    for ref, at_even, at_odd in ((far_ref, 0, 5), (spa_ref, 2, 3), (spb_ref, 5, 0), (sown_ref, 3, 2)):
+        weights.append(weights_of(jnp.where(odd, at_odd, at_even), ref.at[pl.ds(base, 16)], partners_ref))
+
+    def store(row, col, field):
+        field_ref[row, col] = (part_ref[row, col] + field).astype(jnp.bfloat16)
+
+    field_terms(jnp.concatenate(weights, axis=0), [far_ref, spa_ref, spb_ref, sown_ref], blocks, length, store)
 
     span = TILE + LAGS
     steps = length // TILE
@@ -152,7 +174,9 @@
 
 
 VMEM = pl.BlockSpec(memory_space=pltpu.VMEM)
+HBM = pl.BlockSpec(memory_space=pltpu.HBM)
 SMEM = pl.BlockSpec(memory_space=pltpu.SMEM)
+TOTALS_PARAMS = pltpu.CompilerParams(vmem_limit_bytes=54784 * 1024)
 PARAMS = pltpu.CompilerParams(vmem_limit_bytes=VMEM_BYTES)
 
 
@@ -170,43 +194,72 @@
         pairs = [(i, (i + (by_odd if i % 2 else by_even)) % space_size) for i in range(space_size)]
         return lax.ppermute(value, "space", pairs)
 
+    own = pl.pallas_call(
+        totals_kernel,
+        out_shape=jax.ShapeDtypeStruct((2 * rows, length), bf16),
+        in_specs=[HBM, HBM],
+        out_specs=VMEM,
+        scratch_shapes=[
+            pltpu.VMEM((components, molecules, length), bf16),
+            pltpu.VMEM((components, molecules, length), bf16),
+            pltpu.SemaphoreType.DMA((2,)),
+        ],
+        compiler_params=TOTALS_PARAMS,
+        cost_estimate=pl.CostEstimate(flops=4 * 32 * 64 * 3072, bytes_accessed=1200000, transcendentals=0),
+        name="totals",
+    )(dipole_rates.transpose(1, 0, 2), polar_rates.transpose(1, 0, 2))
     pack = pl.pallas_call(
         pack_kernel,
         out_shape=jax.ShapeDtypeStruct((pack_rows, LANE), bf16),
-        in_specs=[SMEM, VMEM, VMEM, VMEM],
-        out_specs=VMEM,
-        compiler_params=PARAMS,
-        cost_estimate=pl.CostEstimate(flops=2 * 32 * 64 * 3072, bytes_accessed=600000, transcendentals=0),
+        grid=(1,),
+        in_specs=[
+            SMEM,
+            pl.BlockSpec((rows, length), lambda i: (0, 0)),
+            pl.BlockSpec((1, space_size), lambda i: (0, 0)),
+            pl.BlockSpec((send_blocks.shape[2], space_size), lambda i: (0, 0)),
+        ],
+        out_specs=pl.BlockSpec((pack_rows, LANE), lambda i: (0, 0)),
+        compiler_params=PARAMS,
+        cost_estimate=pl.CostEstimate(flops=10**10, bytes_accessed=400000, transcendentals=0),
         name="pack",
-    )(domain[None], dipole_rates.transpose(1, 0, 2), pair_counts, send_blocks[0].T)
-    own = pl.pallas_call(
-        own_kernel,
-        out_shape=jax.ShapeDtypeStruct((2 * rows, length), bf16),
-        in_specs=[VMEM, VMEM],
-        out_specs=VMEM,
-        compiler_params=PARAMS,
-        cost_estimate=pl.CostEstimate(flops=2 * 32 * 64 * 3072, bytes_accessed=980000, transcendentals=0),
-        name="own",
-    )(pack, polar_rates.transpose(1, 0, 2))
-
+    )(domain[None], own, pair_counts, send_blocks[0].T)
+
+    following = lax.ppermute(own, "tm", [(i, i - 1) for i in range(1, time_size)])
     pa = moved(pack, -2, 2)
     pb = moved(pack, 2, -2)
-    following = lax.ppermute(own, "tm", [(i, i - 1) for i in range(1, time_size)])
-    sown = moved(pack, 1, -1)
-    far = moved(pa, -1, 1)
-    spa = moved(pa, 1, -1)
-    spb = moved(pb, 1, -1)
-
+    far = moved(pack, -3, 3)
+    joined = pl.pallas_call(
+        join_kernel,
+        out_shape=jax.ShapeDtypeStruct((3 * pack_rows, LANE), bf16),
+        in_specs=[VMEM] * 3,
+        out_specs=VMEM,
+        compiler_params=PARAMS,
+        cost_estimate=pl.CostEstimate(flops=0, bytes_accessed=1200000, transcendentals=0),
+        name="join",
+    )(pack, pa, pb)
+    swapped = moved(joined, 1, -1)
+
+    odd = (domain % 2)[None]
+    pa_later, following = lax.optimization_barrier((pa, following))
+    part = pl.pallas_call(
+        near_kernel,
+        out_shape=jax.ShapeDtypeStruct((rows, length), jnp.float32),
+        in_specs=[SMEM] + [VMEM] * 4,
+        out_specs=VMEM,
+        compiler_params=PARAMS,
+        cost_estimate=pl.CostEstimate(flops=10**10, bytes_accessed=1000000, transcendentals=0),
+        name="near",
+    )(odd, partners.T, pack, pa_later, pb)
     sums = pl.pallas_call(
         sums_kernel,
         out_shape=jax.ShapeDtypeStruct((LAGS // LANE, 4, LANE), jnp.float32),
-        in_specs=[SMEM] + [VMEM] * 10,
+        in_specs=[SMEM] + [VMEM] * 6,
         out_specs=VMEM,
         scratch_shapes=[pltpu.VMEM((rows, length), bf16)],
         compiler_params=PARAMS,
         cost_estimate=pl.CostEstimate(flops=2 * 300000000, bytes_accessed=2500000, transcendentals=0),
         name="sums",
-    )((domain % 2)[None], partners.T, pack, pa, pb, far, spa, spb, sown, own, following)
+    )(odd, partners.T, part, far, swapped, own, following)
 
     shares = lax.all_to_all(sums, "tm", 0, 0)
     lag_share = LAGS // time_size

time: 52.5 us -> 47.7 us (0.909)
  the two profiles are of different devices: /device:TPU:32 before, /device:TPU:1 now
where the time goes in v1:
time: 47.7 us; the launch traced here: 47.4 us
  starting transfers between devices  23.9 us (50%)
  waiting for transfers between devices  17.5 us (37%)
  Pallas kernels  4.56 us (10%)
  local copies, waits for them, and re-layouts  0.65 us (1%)
  other arithmetic  0.61 us (1%)
    ppermute x4, starting transfers between devices, moved(): return lax.ppermute(value, 'space', pairs)  13.9 us
    ppermute x4, waiting for transfers between devices, moved(): return lax.ppermute(value, 'space', pairs)  10.9 us
    all_to_all x1, starting transfers between devices, per_device(): shares = lax.all_to_all(sums, 'tm', 0, 0)  8.69 us
    all_to_all x1, waiting for transfers between devices, per_device(): shares = lax.all_to_all(sums, 'tm', 0, 0)  6.67 us
    pallas_call x1, Pallas kernels, per_device(): pl.pallas_call(sums_kernel, out_shape=jax.ShapeDtypeStruct((LAGS // LANE,...  2.52 us
    pallas_call x1, Pallas kernels, per_device(): pl.pallas_call(totals_kernel, out_shape=jax.ShapeDtypeStruct((2 * rows, l...  1.41 us
    ppermute x1, starting transfers between devices, per_device(): lax.ppermute(own, 'tm', [(i, i - 1) for i in range(1, time_size)])  1.29 us
  transfers between devices with their start and end apart: 6, of which 3 were waited for; matrix products, arithmetic and copies ran while one was open for 0% of the time, Pallas kernels for 1%

profile of v1, /device:TPU:1, one launch (start us, length us, event | category | flops | bytes accessed | tf_op | source)
XLA Modules:
  0.0 47.4 jit_solution(4083503289061267778)
XLA Ops:
  0.0 0.0 copy-start
  0.0 1.4 %totals.1.own_ref = bf16[192,1024]{1,0:T(8,128)(2,1)S(1)} custom-call(bf16[3,64,1024]{2,1,0:T(8,128)(2,1)} %bitcast.13, bf16[3,64,1024]{2,1,0:T(8,128)(2,1)} %bitcast.14), custom_call_target="tpu_custom_call" | custom-call | flops 25165824 | bytes 1200000 | tf_op jit(solution)/shard_map/totals/pallas_call | solution.py:197
  1.4 1.3 %collective-permute-start.1 = (bf16[192,1024]{1,0:T(8,128)(2,1)S(1)}, bf16[192,1024]{1,0:T(8,128)(2,1)S(1)}, u32[]{:S(2)}, u32[]{:S(2)}) collective-permute-start(bf16[192,1024]{1,0:T(8,128)(2,1)S(1)} %totals.1.own_ref), channel_id=1, source_target_pairs={{1,0},{2,1},{3,2},{4,3},{5,4},{6,5},{7,6},{9,8},{10,9},{11,10},{12... | collective-permute-start | bytes 1179656 | tf_op jit(solution)/shard_map/ppermute | solution.py:227
  2.7 0.0 copy-start.2
  2.7 0.0 copy-done
  2.8 0.6 %copy-done.2 = s32[1,64]{1,0:T(1,128)S(1)} copy-done((s32[1,64]{1,0:T(1,128)S(1)}, s32[1,64]{1,0:T(1,128)}, u32[]{:S(2)}) %copy-start.2) | copy-done | bytes 280
  3.4 0.1 pack.1.pack_ref.first_ref
  3.5 8.1 %collective-permute-start.2 = (bf16[784,128]{1,0:T(8,128)(2,1)S(1)}, bf16[784,128]{1,0:T(8,128)(2,1)S(1)}, u32[]{:S(2)}, u32[]{:S(2)}) collective-permute-start(bf16[784,128]{1,0:T(8,128)(2,1)S(1)} %pack.1.pack_ref.first_ref), channel_id=1, source_target_pairs={{0,16},{8,504},{16,32},{24,8},{32,48},{40,24},{48,64},{56,40},{64,... | collective-permute-start | bytes 602120 | tf_op jit(solution)/shard_map/ppermute | solution.py:195
  11.6 1.9 %collective-permute-start = (bf16[784,128]{1,0:T(8,128)(2,1)S(1)}, bf16[784,128]{1,0:T(8,128)(2,1)S(1)}, u32[]{:S(2)}, u32[]{:S(2)}) collective-permute-start(bf16[784,128]{1,0:T(8,128)(2,1)S(1)} %pack.1.pack_ref.first_ref), channel_id=1, source_target_pairs={{0,496},{8,24},{16,0},{24,40},{32,16},{40,56},{48,32},{56,72},{64,... | collective-permute-start | bytes 602120 | tf_op jit(solution)/shard_map/ppermute | solution.py:195
  13.6 1.9 %collective-permute-start.3 = (bf16[784,128]{1,0:T(8,128)(2,1)S(1)}, bf16[784,128]{1,0:T(8,128)(2,1)S(1)}, u32[]{:S(2)}, u32[]{:S(2)}) collective-permute-start(bf16[784,128]{1,0:T(8,128)(2,1)S(1)} %pack.1.pack_ref.first_ref), channel_id=1, source_target_pairs={{0,488},{8,32},{16,504},{24,48},{32,8},{40,64},{48,24},{56,80},{64... | collective-permute-start | bytes 602120 | tf_op jit(solution)/shard_map/ppermute | solution.py:195
  15.5 0.0 copy-start.1
  15.5 0.0 collective-permute-done.2.pb_ref.third_ref
  15.5 9.4 %collective-permute-done.pa_ref.second_ref = bf16[784,128]{1,0:T(8,128)(2,1)S(1)} collective-permute-done((bf16[784,128]{1,0:T(8,128)(2,1)S(1)}, bf16[784,128]{1,0:T(8,128)(2,1)S(1)}, u32[]{:S(2)}, u32[]{:S(2)}) %collective-permute-start) | collective-permute-done | bytes 200736 | tf_op jit(solution)/shard_map/ppermute | solution.py:195
  24.9 1.9 %collective-permute-start.4 = (bf16[2352,128]{1,0:T(8,128)(2,1)S(1)}, bf16[2352,128]{1,0:T(8,128)(2,1)S(1)}, u32[]{:S(2)}, u32[]{:S(2)}) collective-permute-start(bf16[2352,128]{1,0:T(8,128)(2,1)S(1)} %join.1), channel_id=1, source_target_pairs={{0,8},{8,0},{16,24},{24,16},{32,40},{40,32},{48,56},{56,48},{64,72... | collective-permute-start | bytes 1806344 | tf_op jit(solution)/shard_map/ppermute | solution.py:195
  26.9 0.0 collective-permute-done.1.next_ref
  26.9 0.0 copy-done.1
  26.9 0.4 near.1.part_ref
  27.4 0.0 collective-permute-done.3.far_ref
  27.4 1.5 %collective-permute-done.4.swap_ref = bf16[2352,128]{1,0:T(8,128)(2,1)S(1)} collective-permute-done((bf16[2352,128]{1,0:T(8,128)(2,1)S(1)}, bf16[2352,128]{1,0:T(8,128)(2,1)S(1)}, u32[]{:S(2)}, u32[]{:S(2)}) %collective-permute-start.4) | collective-permute-done | bytes 602144 | tf_op jit(solution)/shard_map/ppermute | solution.py:195
  28.9 2.5 %sums.1 = f32[8,4,128]{2,1,0:T(4,128)} custom-call(s32[1]{0:T(128)} %bitcast.odd_ref, s32[24,32]{1,0:T(8,128)S(1)} %bitcast.12, f32[96,1024]{1,0:T(8,128)S(1)} %near.1.part_ref, bf16[784,128]{1,0:T(8,128)(2,1)S(1)} %collective-permute-done.3.far_ref, bf16[2352,128]{1,0:T(8,128)(2,1)S(1)} %collective-permute-done.4.swap_ref, ...), custom_call_target="tpu_custom_call" | custom-call | flops 600000000 | bytes 2500000 | tf_op jit(solution)/shard_map/sums/pallas_call | solution.py:253
  31.4 8.7 %all-to-all-start = ((f32[8,4,128]{2,1,0:T(4,128)}), f32[8,4,128]{2,1,0:T(4,128)S(1)}, u32[]{:S(2)}, u32[]{:S(2)}) async-start(f32[8,4,128]{2,1,0:T(4,128)} %sums.1), calls=%async_computation | async-start | bytes 32768 | tf_op jit(solution)/shard_map/all_to_all | solution.py:264
  40.1 6.7 %all-to-all-done = f32[8,4,128]{2,1,0:T(4,128)S(1)} async-done(((f32[8,4,128]{2,1,0:T(4,128)}), f32[8,4,128]{2,1,0:T(4,128)S(1)}, u32[]{:S(2)}, u32[]{:S(2)}) %all-to-all-start) | async-done | bytes 16416 | tf_op jit(solution)/shard_map/all_to_all | solution.py:264
  46.8 0.6 %bitcast_divide_fusion = f32[1,4,128]{2,1,0:T(4,128)} fusion(f32[4,128]{1,0:T(4,128)S(1)} %reduce_sum.11, f32[128]{0:T(128)S(1)} %subtract_convert_fusion), kind=kLoop, calls=%fused_computation | loop fusion | flops 512 | bytes 4608 | tf_op jit(solution)/shard_map/div | solution.py:268
  (3 shorter events, 0.1 us)
Async XLA Ops:
  0.0 2.7 %copy-start = (s32[1,64,24]{1,2,0:T(8,128)S(1)}, s32[1,64,24]{1,2,0:T(8,128)}, u32[]{:S(2)}) copy-start(s32[1,64,24]{1,2,0:T(8,128)} %param.8) | copy-start | bytes 18436
  1.4 25.5 %collective-permute-start.1 = (bf16[192,1024]{1,0:T(8,128)(2,1)S(1)}, bf16[192,1024]{1,0:T(8,128)(2,1)S(1)}, u32[]{:S(2)}, u32[]{:S(2)}) collective-permute-start(bf16[192,1024]{1,0:T(8,128)(2,1)S(1)} %totals.1.own_ref), channel_id=1, source_target_pairs={{1,0},{2,1},{3,2},{4,3},{5,4},{6,5},{7,6},{9,8},{10,9},{11,10},{12... | collective-permute-start | bytes 1179656 | tf_op jit(solution)/shard_map/ppermute | solution.py:227
  2.7 0.7 %copy-start.2 = (s32[1,64]{1,0:T(1,128)S(1)}, s32[1,64]{1,0:T(1,128)}, u32[]{:S(2)}) copy-start(s32[1,64]{1,0:T(1,128)} %counts_ref.1) | copy-start | bytes 772
  3.5 12.0 %collective-permute-start.2 = (bf16[784,128]{1,0:T(8,128)(2,1)S(1)}, bf16[784,128]{1,0:T(8,128)(2,1)S(1)}, u32[]{:S(2)}, u32[]{:S(2)}) collective-permute-start(bf16[784,128]{1,0:T(8,128)(2,1)S(1)} %pack.1.pack_ref.first_ref), channel_id=1, source_target_pairs={{0,16},{8,504},{16,32},{24,8},{32,48},{40,24},{48,64},{56,40},{64,... | collective-permute-start | bytes 602120 | tf_op jit(solution)/shard_map/ppermute | solution.py:195
  11.6 13.3 %collective-permute-start = (bf16[784,128]{1,0:T(8,128)(2,1)S(1)}, bf16[784,128]{1,0:T(8,128)(2,1)S(1)}, u32[]{:S(2)}, u32[]{:S(2)}) collective-permute-start(bf16[784,128]{1,0:T(8,128)(2,1)S(1)} %pack.1.pack_ref.first_ref), channel_id=1, source_target_pairs={{0,496},{8,24},{16,0},{24,40},{32,16},{40,56},{48,32},{56,72},{64,... | collective-permute-start | bytes 602120 | tf_op jit(solution)/shard_map/ppermute | solution.py:195
  13.6 13.8 %collective-permute-start.3 = (bf16[784,128]{1,0:T(8,128)(2,1)S(1)}, bf16[784,128]{1,0:T(8,128)(2,1)S(1)}, u32[]{:S(2)}, u32[]{:S(2)}) collective-permute-start(bf16[784,128]{1,0:T(8,128)(2,1)S(1)} %pack.1.pack_ref.first_ref), channel_id=1, source_target_pairs={{0,488},{8,32},{16,504},{24,48},{32,8},{40,64},{48,24},{56,80},{64... | collective-permute-start | bytes 602120 | tf_op jit(solution)/shard_map/ppermute | solution.py:195
  15.5 11.4 %copy-start.1 = (s32[32,24]{0,1:T(8,128)S(1)}, s32[32,24]{0,1:T(8,128)}, u32[]{:S(2)}) copy-start(s32[32,24]{0,1:T(8,128)} %param.9) | copy-start | bytes 9220
  24.9 3.9 %collective-permute-start.4 = (bf16[2352,128]{1,0:T(8,128)(2,1)S(1)}, bf16[2352,128]{1,0:T(8,128)(2,1)S(1)}, u32[]{:S(2)}, u32[]{:S(2)}) collective-permute-start(bf16[2352,128]{1,0:T(8,128)(2,1)S(1)} %join.1), channel_id=1, source_target_pairs={{0,8},{8,0},{16,24},{24,16},{32,40},{40,32},{48,56},{56,48},{64,72... | collective-permute-start | bytes 1806344 | tf_op jit(solution)/shard_map/ppermute | solution.py:195
  31.4 15.4 %all-to-all-start = ((f32[8,4,128]{2,1,0:T(4,128)}), f32[8,4,128]{2,1,0:T(4,128)S(1)}, u32[]{:S(2)}, u32[]{:S(2)}) async-start(f32[8,4,128]{2,1,0:T(4,128)} %sums.1), calls=%async_computation | async-start | bytes 32768 | tf_op jit(solution)/shard_map/all_to_all | solution.py:264

commit v2 on v1

--- a/solution.py
+++ b/solution.py
@@ -60,6 +60,10 @@
     pack_ref[base : base + 16, :] = meta.astype(jnp.bfloat16)
 
 
+def touch_kernel(a_ref, b_ref):
+    b_ref[...] = a_ref[...]
+
+
 def join_kernel(first_ref, second_ref, third_ref, joined_ref):
     count = first_ref.shape[0]
     for i, ref in enumerate((first_ref, second_ref, third_ref)):
@@ -220,21 +224,30 @@
         ],
         out_specs=pl.BlockSpec((pack_rows, LANE), lambda i: (0, 0)),
         compiler_params=PARAMS,
-        cost_estimate=pl.CostEstimate(flops=10**10, bytes_accessed=400000, transcendentals=0),
+        cost_estimate=pl.CostEstimate(flops=10**6, bytes_accessed=400000, transcendentals=0),
         name="pack",
     )(domain[None], own, pair_counts, send_blocks[0].T)
 
     following = lax.ppermute(own, "tm", [(i, i - 1) for i in range(1, time_size)])
     pa = moved(pack, -2, 2)
     pb = moved(pack, 2, -2)
-    far = moved(pack, -3, 3)
+    far_pack = pl.pallas_call(
+        touch_kernel,
+        out_shape=jax.ShapeDtypeStruct((pack_rows, LANE), bf16),
+        in_specs=[VMEM],
+        out_specs=VMEM,
+        compiler_params=PARAMS,
+        cost_estimate=pl.CostEstimate(flops=10**6, bytes_accessed=400000, transcendentals=0),
+        name="touch",
+    )(pack)
+    far = moved(far_pack, -3, 3)
     joined = pl.pallas_call(
         join_kernel,
         out_shape=jax.ShapeDtypeStruct((3 * pack_rows, LANE), bf16),
         in_specs=[VMEM] * 3,
         out_specs=VMEM,
         compiler_params=PARAMS,
-        cost_estimate=pl.CostEstimate(flops=0, bytes_accessed=1200000, transcendentals=0),
+        cost_estimate=pl.CostEstimate(flops=3*10**9, bytes_accessed=1200000, transcendentals=0),
         name="join",
     )(pack, pa, pb)
     swapped = moved(joined, 1, -1)

time: 47.7 us -> 46.1 us (0.966)
  the two profiles are of different devices: /device:TPU:1 before, /device:TPU:32 now
where the time goes in v2:
time: 46.1 us; the launch traced here: 45.8 us
  starting transfers between devices  27.3 us (59%)
  waiting for transfers between devices  12.5 us (27%)
  Pallas kernels  4.56 us (10%)
  local copies, waits for them, and re-layouts  0.65 us (1%)
  other arithmetic  0.61 us (1%)
    ppermute x4, starting transfers between devices, moved(): return lax.ppermute(value, 'space', pairs)  14.5 us
    all_to_all x1, starting transfers between devices, per_device(): shares = lax.all_to_all(sums, 'tm', 0, 0)  11.5 us
    all_to_all x1, waiting for transfers between devices, per_device(): shares = lax.all_to_all(sums, 'tm', 0, 0)  7.77 us
    ppermute x1, waiting for transfers between devices, per_device(): lax.ppermute(own, 'tm', [(i, i - 1) for i in range(1, time_size)])  3.61 us
    pallas_call x1, Pallas kernels, per_device(): pl.pallas_call(sums_kernel, out_shape=jax.ShapeDtypeStruct((LAGS // LANE,...  2.52 us
    pallas_call x1, Pallas kernels, per_device(): pl.pallas_call(totals_kernel, out_shape=jax.ShapeDtypeStruct((2 * rows, l...  1.41 us
    ppermute x1, starting transfers between devices, per_device(): lax.ppermute(own, 'tm', [(i, i - 1) for i in range(1, time_size)])  1.29 us
    ppermute x4, waiting for transfers between devices, moved(): return lax.ppermute(value, 'space', pairs)  1.1 us
  transfers between devices with their start and end apart: 6, of which 3 were waited for; matrix products, arithmetic and copies ran while one was open for 0% of the time, Pallas kernels for 1%

profile of v2, /device:TPU:32, one launch (start us, length us, event | category | flops | bytes accessed | tf_op | source)
XLA Modules:
  0.0 45.8 jit_solution(15970400682668452580)
XLA Ops:
  0.0 0.0 copy-start
  0.0 1.4 %totals.1.own_ref = bf16[192,1024]{1,0:T(8,128)(2,1)S(1)} custom-call(bf16[3,64,1024]{2,1,0:T(8,128)(2,1)} %bitcast.13, bf16[3,64,1024]{2,1,0:T(8,128)(2,1)} %bitcast.14), custom_call_target="tpu_custom_call" | custom-call | flops 25165824 | bytes 1200000 | tf_op jit(solution)/shard_map/totals/pallas_call | solution.py:201
  1.4 0.0 copy-start.1
  1.4 0.0 copy-done
  1.4 0.6 %copy-done.1 = s32[1,64]{1,0:T(1,128)S(1)} copy-done((s32[1,64]{1,0:T(1,128)S(1)}, s32[1,64]{1,0:T(1,128)}, u32[]{:S(2)}) %copy-start.1) | copy-done | bytes 280
  2.1 0.1 pack.1.pack_ref.a_ref.first_ref
  2.2 3.4 %collective-permute-start.2 = (bf16[784,128]{1,0:T(8,128)(2,1)S(1)}, bf16[784,128]{1,0:T(8,128)(2,1)S(1)}, u32[]{:S(2)}, u32[]{:S(2)}) collective-permute-start(bf16[784,128]{1,0:T(8,128)(2,1)S(1)} %pack.1.pack_ref.a_ref.first_ref), channel_id=1, source_target_pairs={{0,16},{8,504},{16,32},{24,8},{32,48},{40,24},{48,64},{56,40},{64,... | collective-permute-start | bytes 602120 | tf_op jit(solution)/shard_map/ppermute | solution.py:199
  5.6 5.8 %collective-permute-start = (bf16[784,128]{1,0:T(8,128)(2,1)S(1)}, bf16[784,128]{1,0:T(8,128)(2,1)S(1)}, u32[]{:S(2)}, u32[]{:S(2)}) collective-permute-start(bf16[784,128]{1,0:T(8,128)(2,1)S(1)} %pack.1.pack_ref.a_ref.first_ref), channel_id=1, source_target_pairs={{0,496},{8,24},{16,0},{24,40},{32,16},{40,56},{48,32},{56,72},{64,... | collective-permute-start | bytes 602120 | tf_op jit(solution)/shard_map/ppermute | solution.py:199
  11.4 1.3 %collective-permute-start.1 = (bf16[192,1024]{1,0:T(8,128)(2,1)S(1)}, bf16[192,1024]{1,0:T(8,128)(2,1)S(1)}, u32[]{:S(2)}, u32[]{:S(2)}) collective-permute-start(bf16[192,1024]{1,0:T(8,128)(2,1)S(1)} %totals.1.own_ref), channel_id=1, source_target_pairs={{1,0},{2,1},{3,2},{4,3},{5,4},{6,5},{7,6},{9,8},{10,9},{11,10},{12... | collective-permute-start | bytes 1179656 | tf_op jit(solution)/shard_map/ppermute | solution.py:231
  12.7 1.9 %collective-permute-start.3 = (bf16[784,128]{1,0:T(8,128)(2,1)S(1)}, bf16[784,128]{1,0:T(8,128)(2,1)S(1)}, u32[]{:S(2)}, u32[]{:S(2)}) collective-permute-start(bf16[784,128]{1,0:T(8,128)(2,1)S(1)} %touch.1), channel_id=1, source_target_pairs={{0,488},{8,32},{16,504},{24,48},{32,8},{40,64},{48,24},{56,80},{64... | collective-permute-start | bytes 602120 | tf_op jit(solution)/shard_map/ppermute | solution.py:199
  14.6 0.0 copy-start.2
  14.7 0.0 collective-permute-done.2.pb_ref.third_ref
  14.7 0.0 collective-permute-done.pa_ref.second_ref
  14.7 3.5 %collective-permute-start.4 = (bf16[2352,128]{1,0:T(8,128)(2,1)S(1)}, bf16[2352,128]{1,0:T(8,128)(2,1)S(1)}, u32[]{:S(2)}, u32[]{:S(2)}) collective-permute-start(bf16[2352,128]{1,0:T(8,128)(2,1)S(1)} %join.1), channel_id=1, source_target_pairs={{0,8},{8,0},{16,24},{24,16},{32,40},{40,32},{48,56},{56,48},{64,72... | collective-permute-start | bytes 1806344 | tf_op jit(solution)/shard_map/ppermute | solution.py:199
  18.2 3.6 %collective-permute-done.1.next_ref = bf16[192,1024]{1,0:T(8,128)(2,1)S(1)} collective-permute-done((bf16[192,1024]{1,0:T(8,128)(2,1)S(1)}, bf16[192,1024]{1,0:T(8,128)(2,1)S(1)}, u32[]{:S(2)}, u32[]{:S(2)}) %collective-permute-start.1) | collective-permute-done | bytes 393248 | tf_op jit(solution)/shard_map/ppermute | solution.py:231
  21.8 0.0 copy-done.2
  21.8 0.4 near.1.part_ref
  22.3 1.1 %collective-permute-done.3.far_ref = bf16[784,128]{1,0:T(8,128)(2,1)S(1)} collective-permute-done((bf16[784,128]{1,0:T(8,128)(2,1)S(1)}, bf16[784,128]{1,0:T(8,128)(2,1)S(1)}, u32[]{:S(2)}, u32[]{:S(2)}) %collective-permute-start.3) | collective-permute-done | bytes 200736 | tf_op jit(solution)/shard_map/ppermute | solution.py:199
  23.4 0.0 collective-permute-done.4.swap_ref
  23.4 2.5 %sums.1 = f32[8,4,128]{2,1,0:T(4,128)} custom-call(s32[1]{0:T(128)} %bitcast.odd_ref, s32[24,32]{1,0:T(8,128)S(1)} %bitcast.12, f32[96,1024]{1,0:T(8,128)S(1)} %near.1.part_ref, bf16[784,128]{1,0:T(8,128)(2,1)S(1)} %collective-permute-done.3.far_ref, bf16[2352,128]{1,0:T(8,128)(2,1)S(1)} %collective-permute-done.4.swap_ref, ...), custom_call_target="tpu_custom_call" | custom-call | flops 600000000 | bytes 2500000 | tf_op jit(solution)/shard_map/sums/pallas_call | solution.py:266
  25.9 11.5 %all-to-all-start = ((f32[8,4,128]{2,1,0:T(4,128)}), f32[8,4,128]{2,1,0:T(4,128)S(1)}, u32[]{:S(2)}, u32[]{:S(2)}) async-start(f32[8,4,128]{2,1,0:T(4,128)} %sums.1), calls=%async_computation | async-start | bytes 32768 | tf_op jit(solution)/shard_map/all_to_all | solution.py:277
  37.4 7.8 %all-to-all-done = f32[8,4,128]{2,1,0:T(4,128)S(1)} async-done(((f32[8,4,128]{2,1,0:T(4,128)}), f32[8,4,128]{2,1,0:T(4,128)S(1)}, u32[]{:S(2)}, u32[]{:S(2)}) %all-to-all-start) | async-done | bytes 16416 | tf_op jit(solution)/shard_map/all_to_all | solution.py:277
  45.2 0.6 %bitcast_divide_fusion = f32[1,4,128]{2,1,0:T(4,128)} fusion(f32[4,128]{1,0:T(4,128)S(1)} %reduce_sum.11, f32[128]{0:T(128)S(1)} %subtract_convert_fusion), kind=kLoop, calls=%fused_computation | loop fusion | flops 512 | bytes 4608 | tf_op jit(solution)/shard_map/div | solution.py:281
  (4 shorter events, 0.1 us)
Async XLA Ops:
  0.0 1.4 %copy-start = (s32[1,64,24]{1,2,0:T(8,128)S(1)}, s32[1,64,24]{1,2,0:T(8,128)}, u32[]{:S(2)}) copy-start(s32[1,64,24]{1,2,0:T(8,128)} %param.8) | copy-start | bytes 18436
  1.4 0.7 %copy-start.1 = (s32[1,64]{1,0:T(1,128)S(1)}, s32[1,64]{1,0:T(1,128)}, u32[]{:S(2)}) copy-start(s32[1,64]{1,0:T(1,128)} %counts_ref.1) | copy-start | bytes 772
  2.2 12.4 %collective-permute-start.2 = (bf16[784,128]{1,0:T(8,128)(2,1)S(1)}, bf16[784,128]{1,0:T(8,128)(2,1)S(1)}, u32[]{:S(2)}, u32[]{:S(2)}) collective-permute-start(bf16[784,128]{1,0:T(8,128)(2,1)S(1)} %pack.1.pack_ref.a_ref.first_ref), channel_id=1, source_target_pairs={{0,16},{8,504},{16,32},{24,8},{32,48},{40,24},{48,64},{56,40},{64,... | collective-permute-start | bytes 602120 | tf_op jit(solution)/shard_map/ppermute | solution.py:199
  5.6 9.1 %collective-permute-start = (bf16[784,128]{1,0:T(8,128)(2,1)S(1)}, bf16[784,128]{1,0:T(8,128)(2,1)S(1)}, u32[]{:S(2)}, u32[]{:S(2)}) collective-permute-start(bf16[784,128]{1,0:T(8,128)(2,1)S(1)} %pack.1.pack_ref.a_ref.first_ref), channel_id=1, source_target_pairs={{0,496},{8,24},{16,0},{24,40},{32,16},{40,56},{48,32},{56,72},{64,... | collective-permute-start | bytes 602120 | tf_op jit(solution)/shard_map/ppermute | solution.py:199
  11.4 10.4 %collective-permute-start.1 = (bf16[192,1024]{1,0:T(8,128)(2,1)S(1)}, bf16[192,1024]{1,0:T(8,128)(2,1)S(1)}, u32[]{:S(2)}, u32[]{:S(2)}) collective-permute-start(bf16[192,1024]{1,0:T(8,128)(2,1)S(1)} %totals.1.own_ref), channel_id=1, source_target_pairs={{1,0},{2,1},{3,2},{4,3},{5,4},{6,5},{7,6},{9,8},{10,9},{11,10},{12... | collective-permute-start | bytes 1179656 | tf_op jit(solution)/shard_map/ppermute | solution.py:231
  12.7 10.6 %collective-permute-start.3 = (bf16[784,128]{1,0:T(8,128)(2,1)S(1)}, bf16[784,128]{1,0:T(8,128)(2,1)S(1)}, u32[]{:S(2)}, u32[]{:S(2)}) collective-permute-start(bf16[784,128]{1,0:T(8,128)(2,1)S(1)} %touch.1), channel_id=1, source_target_pairs={{0,488},{8,32},{16,504},{24,48},{32,8},{40,64},{48,24},{56,80},{64... | collective-permute-start | bytes 602120 | tf_op jit(solution)/shard_map/ppermute | solution.py:199
  14.6 7.2 %copy-start.2 = (s32[32,24]{0,1:T(8,128)S(1)}, s32[32,24]{0,1:T(8,128)}, u32[]{:S(2)}) copy-start(s32[32,24]{0,1:T(8,128)} %param.9) | copy-start | bytes 9220
  14.7 8.6 %collective-permute-start.4 = (bf16[2352,128]{1,0:T(8,128)(2,1)S(1)}, bf16[2352,128]{1,0:T(8,128)(2,1)S(1)}, u32[]{:S(2)}, u32[]{:S(2)}) collective-permute-start(bf16[2352,128]{1,0:T(8,128)(2,1)S(1)} %join.1), channel_id=1, source_target_pairs={{0,8},{8,0},{16,24},{24,16},{32,40},{40,32},{48,56},{56,48},{64,72... | collective-permute-start | bytes 1806344 | tf_op jit(solution)/shard_map/ppermute | solution.py:199
  25.9 19.3 %all-to-all-start = ((f32[8,4,128]{2,1,0:T(4,128)}), f32[8,4,128]{2,1,0:T(4,128)S(1)}, u32[]{:S(2)}, u32[]{:S(2)}) async-start(f32[8,4,128]{2,1,0:T(4,128)} %sums.1), calls=%async_computation | async-start | bytes 32768 | tf_op jit(solution)/shard_map/all_to_all | solution.py:277

commit v3 on v2

--- a/solution.py
+++ b/solution.py
@@ -60,14 +60,8 @@
     pack_ref[base : base + 16, :] = meta.astype(jnp.bfloat16)
 
 
-def touch_kernel(a_ref, b_ref):
+def touch_kernel(a_ref, unused_ref, b_ref):
     b_ref[...] = a_ref[...]
-
-
-def join_kernel(first_ref, second_ref, third_ref, joined_ref):
-    count = first_ref.shape[0]
-    for i, ref in enumerate((first_ref, second_ref, third_ref)):
-        joined_ref[i * count : (i + 1) * count, :] = ref[...]
 
 
 def fold(gram):
@@ -121,19 +115,26 @@
             store(slice(c * blocks, (c + 1) * blocks), slice(j * LANE, (j + 2) * LANE), field)
 
 
-def near_kernel(odd_ref, partners_ref, pack_ref, pa_ref, pb_ref, part_ref):
+def near_kernel(odd_ref, partners_ref, both_ref, side_ref, part_ref):
     slots, blocks = partners_ref.shape
     rows, length = part_ref.shape
     base = rows * (length // LANE)
+    count = base + 16
     odd = odd_ref[0] == 1
-    weights = [named_by(0, partners_ref).astype(jnp.bfloat16)]
-    for ref, at_even, at_odd in ((pa_ref, 4, 1), (pb_ref, 1, 4)):
+    mine = named_by(0, partners_ref).astype(jnp.bfloat16)
+    refs = [both_ref.at[pl.ds(0, count)], both_ref.at[pl.ds(count, count)]]
+    refs += [side_ref.at[pl.ds(0, count)], side_ref.at[pl.ds(count, count)]]
+    weights = [
+        jnp.where(odd, weights_of(2, refs[0].at[pl.ds(base, 16)], partners_ref), mine),
+        jnp.where(odd, mine, weights_of(3, refs[1].at[pl.ds(base, 16)], partners_ref)),
+    ]
+    for ref, at_even, at_odd in ((refs[2], 1, 3), (refs[3], 2, 4)):
         weights.append(weights_of(jnp.where(odd, at_odd, at_even), ref.at[pl.ds(base, 16)], partners_ref))
 
     def store(row, col, field):
         part_ref[row, col] = field
 
-    field_terms(jnp.concatenate(weights, axis=0), [pack_ref, pa_ref, pb_ref], blocks, length, store)
+    field_terms(jnp.concatenate(weights, axis=0), refs, blocks, length, store)
 
 
 def sums_kernel(odd_ref, partners_ref, part_ref, far_ref, swap_ref, own_ref, next_ref, out_ref, field_ref):
@@ -143,15 +144,15 @@
     base = rows * (length // LANE)
     odd = odd_ref[0] == 1
     count = far_ref.shape[0]
-    sown_ref, spa_ref, spb_ref = [swap_ref.at[pl.ds(i * count, count)] for i in range(3)]
+    refs = [far_ref, swap_ref.at[pl.ds(0, count)], swap_ref.at[pl.ds(count, count)]]
     weights = []
-    for ref, at_even, at_odd in ((far_ref, 0, 5), (spa_ref, 2, 3), (spb_ref, 5, 0), (sown_ref, 3, 2)):
+    for ref, at_even, at_odd in zip(refs, (0, 4, 5), (5, 0, 1)):
         weights.append(weights_of(jnp.where(odd, at_odd, at_even), ref.at[pl.ds(base, 16)], partners_ref))
 
     def store(row, col, field):
         field_ref[row, col] = (part_ref[row, col] + field).astype(jnp.bfloat16)
 
-    field_terms(jnp.concatenate(weights, axis=0), [far_ref, spa_ref, spb_ref, sown_ref], blocks, length, store)
+    field_terms(jnp.concatenate(weights, axis=0), refs, blocks, length, store)
 
     span = TILE + LAGS
     steps = length // TILE
@@ -228,41 +229,34 @@
         name="pack",
     )(domain[None], own, pair_counts, send_blocks[0].T)
 
-    following = lax.ppermute(own, "tm", [(i, i - 1) for i in range(1, time_size)])
-    pa = moved(pack, -2, 2)
-    pb = moved(pack, 2, -2)
+    pairs = [[2 * i, 2 * i + 1] for i in range(space_size // 2)]
+    both = lax.all_gather(pack, "space", axis_index_groups=pairs, tiled=True)
+    own_later = own
+    side = moved(both, -1, 1)
+    following = lax.ppermute(own_later, "tm", [(i, i - 1) for i in range(1, time_size)])
     far_pack = pl.pallas_call(
         touch_kernel,
         out_shape=jax.ShapeDtypeStruct((pack_rows, LANE), bf16),
-        in_specs=[VMEM],
+        in_specs=[VMEM, HBM],
         out_specs=VMEM,
         compiler_params=PARAMS,
         cost_estimate=pl.CostEstimate(flops=10**6, bytes_accessed=400000, transcendentals=0),
         name="touch",
-    )(pack)
+    )(pack, both)
     far = moved(far_pack, -3, 3)
-    joined = pl.pallas_call(
-        join_kernel,
-        out_shape=jax.ShapeDtypeStruct((3 * pack_rows, LANE), bf16),
-        in_specs=[VMEM] * 3,
-        out_specs=VMEM,
-        compiler_params=PARAMS,
-        cost_estimate=pl.CostEstimate(flops=3*10**9, bytes_accessed=1200000, transcendentals=0),
-        name="join",
-    )(pack, pa, pb)
-    swapped = moved(joined, 1, -1)
+    swapped = moved(side, 1, -1)
 
     odd = (domain % 2)[None]
-    pa_later, following = lax.optimization_barrier((pa, following))
+    side_later = side
     part = pl.pallas_call(
         near_kernel,
         out_shape=jax.ShapeDtypeStruct((rows, length), jnp.float32),
-        in_specs=[SMEM] + [VMEM] * 4,
+        in_specs=[SMEM] + [VMEM] * 3,
         out_specs=VMEM,
         compiler_params=PARAMS,
         cost_estimate=pl.CostEstimate(flops=10**10, bytes_accessed=1000000, transcendentals=0),
         name="near",
-    )(odd, partners.T, pack, pa_later, pb)
+    )(odd, partners.T, both, side_later)
     sums = pl.pallas_call(
         sums_kernel,
         out_shape=jax.ShapeDtypeStruct((LAGS // LANE, 4, LANE), jnp.float32),

time: 46.1 us -> 44.5 us (0.965)
  the two profiles are of different devices: /device:TPU:32 before, /device:TPU:64 now
where the time goes in v3:
time: 44.5 us; the launch traced here: 44.2 us
  starting transfers between devices  25 us (56%)
  waiting for transfers between devices  11.2 us (25%)
  Pallas kernels  4.58 us (10%)
  blocking collectives  2.08 us (5%)
  local copies, waits for them, and re-layouts  0.65 us (1%)
  other arithmetic  0.61 us (1%)
    ppermute x3, starting transfers between devices, moved(): return lax.ppermute(value, 'space', pairs)  12.6 us
    all_to_all x1, starting transfers between devices, per_device(): shares = lax.all_to_all(sums, 'tm', 0, 0)  10.5 us
    all_to_all x1, waiting for transfers between devices, per_device(): shares = lax.all_to_all(sums, 'tm', 0, 0)  6.36 us
    ppermute x3, waiting for transfers between devices, moved(): return lax.ppermute(value, 'space', pairs)  4.79 us
    pallas_call x1, Pallas kernels, per_device(): pl.pallas_call(sums_kernel, out_shape=jax.ShapeDtypeStruct((LAGS // LANE,...  2.47 us
    all_gather x1, blocking collectives, per_device(): both = lax.all_gather(pack, 'space', axis_index_groups=pairs, tiled=True)  2.08 us
    ppermute x1, starting transfers between devices, per_device(): lax.ppermute(own_later, 'tm', [(i, i - 1) for i in range(1, time_size)])  1.92 us
    pallas_call x1, Pallas kernels, per_device(): pl.pallas_call(totals_kernel, out_shape=jax.ShapeDtypeStruct((2 * rows, l...  1.41 us
  transfers between devices with their start and end apart: 5, of which 3 were waited for; matrix products, arithmetic and copies ran while one was open for 0% of the time, Pallas kernels for 1%

profile of v3, /device:TPU:64, one launch (start us, length us, event | category | flops | bytes accessed | tf_op | source)
XLA Modules:
  0.0 44.2 jit_solution(1574002350720821515)
XLA Ops:
  0.0 0.0 copy-start
  0.0 1.4 %totals.1.own_ref = bf16[192,1024]{1,0:T(8,128)(2,1)S(1)} custom-call(bf16[3,64,1024]{2,1,0:T(8,128)(2,1)} %bitcast.13, bf16[3,64,1024]{2,1,0:T(8,128)(2,1)} %bitcast.14), custom_call_target="tpu_custom_call" | custom-call | flops 25165824 | bytes 1200000 | tf_op jit(solution)/shard_map/totals/pallas_call | solution.py:202
  1.4 0.0 copy-start.1
  1.4 0.0 copy-done
  1.4 0.6 %copy-done.1 = s32[1,64]{1,0:T(1,128)S(1)} copy-done((s32[1,64]{1,0:T(1,128)S(1)}, s32[1,64]{1,0:T(1,128)}, u32[]{:S(2)}) %copy-start.1) | copy-done | bytes 280
  2.1 0.1 pack.1.a_ref
  2.2 2.1 %all_gather.3.both_ref.unused_ref = bf16[1568,128]{1,0:T(8,128)(2,1)S(1)} all-gather(bf16[784,128]{1,0:T(8,128)(2,1)S(1)} %pack.1.a_ref), channel_id=1, replica_groups={{0,8},{16,24},{32,40},{48,56},{64,72},{80,88},{96,104},{112,120},{128,1..., dimensions={0}, use_global_device_ids=true | all-gather | bytes 602112 | tf_op jit(solution)/shard_map/all_gather | solution.py:233
  4.3 7.3 %collective-permute-start = (bf16[1568,128]{1,0:T(8,128)(2,1)S(1)}, bf16[1568,128]{1,0:T(8,128)(2,1)S(1)}, u32[]{:S(2)}, u32[]{:S(2)}) collective-permute-start(bf16[1568,128]{1,0:T(8,128)(2,1)S(1)} %all_gather.3.both_ref.unused_ref), channel_id=1, source_target_pairs={{0,504},{8,16},{16,8},{24,32},{32,24},{40,48},{48,40},{56,64},{64,... | collective-permute-start | bytes 1204232 | tf_op jit(solution)/shard_map/ppermute | solution.py:200
  11.6 1.9 %collective-permute-start.3 = (bf16[192,1024]{1,0:T(8,128)(2,1)S(1)}, bf16[192,1024]{1,0:T(8,128)(2,1)S(1)}, u32[]{:S(2)}, u32[]{:S(2)}) collective-permute-start(bf16[192,1024]{1,0:T(8,128)(2,1)S(1)} %totals.1.own_ref), channel_id=1, source_target_pairs={{1,0},{2,1},{3,2},{4,3},{5,4},{6,5},{7,6},{9,8},{10,9},{11,10},{12... | collective-permute-start | bytes 1179656 | tf_op jit(solution)/shard_map/ppermute | solution.py:236
  13.6 3.3 %collective-permute-start.1 = (bf16[784,128]{1,0:T(8,128)(2,1)S(1)}, bf16[784,128]{1,0:T(8,128)(2,1)S(1)}, u32[]{:S(2)}, u32[]{:S(2)}) collective-permute-start(bf16[784,128]{1,0:T(8,128)(2,1)S(1)} %touch.1), channel_id=1, source_target_pairs={{0,488},{8,32},{16,504},{24,48},{32,8},{40,64},{48,24},{56,80},{64... | collective-permute-start | bytes 602120 | tf_op jit(solution)/shard_map/ppermute | solution.py:200
  16.9 0.0 copy-start.2
  16.9 0.2 collective-permute-done.side_ref
  17.1 1.9 %collective-permute-start.2 = (bf16[1568,128]{1,0:T(8,128)(2,1)S(1)}, bf16[1568,128]{1,0:T(8,128)(2,1)S(1)}, u32[]{:S(2)}, u32[]{:S(2)}) collective-permute-start(bf16[1568,128]{1,0:T(8,128)(2,1)S(1)} %collective-permute-done.side_ref), channel_id=1, source_target_pairs={{0,8},{8,0},{16,24},{24,16},{32,40},{40,32},{48,56},{56,48},{64,72... | collective-permute-start | bytes 1204232 | tf_op jit(solution)/shard_map/ppermute | solution.py:200
  19.1 0.0 copy-done.2
  19.1 0.5 %near.1.part_ref = f32[96,1024]{1,0:T(8,128)S(1)} custom-call(s32[1]{0:T(128)} %bitcast.odd_ref, s32[24,32]{1,0:T(8,128)S(1)} %bitcast.11, bf16[1568,128]{1,0:T(8,128)(2,1)S(1)} %all_gather.3.both_ref.unused_ref, bf16[1568,128]{1,0:T(8,128)(2,1)S(1)} %collective-permute-done.side_ref), custom_call_target="tpu_custom_call" | custom-call | flops 10000000000 | bytes 1000000 | tf_op jit(solution)/shard_map/near/pallas_call | solution.py:251
  19.6 4.6 %collective-permute-done.1.far_ref = bf16[784,128]{1,0:T(8,128)(2,1)S(1)} collective-permute-done((bf16[784,128]{1,0:T(8,128)(2,1)S(1)}, bf16[784,128]{1,0:T(8,128)(2,1)S(1)}, u32[]{:S(2)}, u32[]{:S(2)}) %collective-permute-start.1) | collective-permute-done | bytes 200736 | tf_op jit(solution)/shard_map/ppermute | solution.py:200
  24.2 0.0 collective-permute-done.3.next_ref
  24.2 0.0 collective-permute-done.2.swap_ref
  24.2 2.5 %sums.1 = f32[8,4,128]{2,1,0:T(4,128)} custom-call(s32[1]{0:T(128)} %bitcast.odd_ref, s32[24,32]{1,0:T(8,128)S(1)} %bitcast.12, f32[96,1024]{1,0:T(8,128)S(1)} %near.1.part_ref, bf16[784,128]{1,0:T(8,128)(2,1)S(1)} %collective-permute-done.1.far_ref, bf16[1568,128]{1,0:T(8,128)(2,1)S(1)} %collective-permute-done.2.swap_ref, ...), custom_call_target="tpu_custom_call" | custom-call | flops 600000000 | bytes 2500000 | tf_op jit(solution)/shard_map/sums/pallas_call | solution.py:260
  26.7 10.5 %all-to-all-start = ((f32[8,4,128]{2,1,0:T(4,128)}), f32[8,4,128]{2,1,0:T(4,128)S(1)}, u32[]{:S(2)}, u32[]{:S(2)}) async-start(f32[8,4,128]{2,1,0:T(4,128)} %sums.1), calls=%async_computation | async-start | bytes 32768 | tf_op jit(solution)/shard_map/all_to_all | solution.py:271
  37.2 6.4 %all-to-all-done = f32[8,4,128]{2,1,0:T(4,128)S(1)} async-done(((f32[8,4,128]{2,1,0:T(4,128)}), f32[8,4,128]{2,1,0:T(4,128)S(1)}, u32[]{:S(2)}, u32[]{:S(2)}) %all-to-all-start) | async-done | bytes 16416 | tf_op jit(solution)/shard_map/all_to_all | solution.py:271
  43.6 0.6 %bitcast_divide_fusion = f32[1,4,128]{2,1,0:T(4,128)} fusion(f32[4,128]{1,0:T(4,128)S(1)} %reduce_sum.11, f32[128]{0:T(128)S(1)} %subtract_convert_fusion), kind=kLoop, calls=%fused_computation | loop fusion | flops 512 | bytes 4608 | tf_op jit(solution)/shard_map/div | solution.py:275
  (3 shorter events, 0.0 us)
Async XLA Ops:
  0.0 1.4 %copy-start = (s32[1,64,24]{1,2,0:T(8,128)S(1)}, s32[1,64,24]{1,2,0:T(8,128)}, u32[]{:S(2)}) copy-start(s32[1,64,24]{1,2,0:T(8,128)} %param.8) | copy-start | bytes 18436
  1.4 0.7 %copy-start.1 = (s32[1,64]{1,0:T(1,128)S(1)}, s32[1,64]{1,0:T(1,128)}, u32[]{:S(2)}) copy-start(s32[1,64]{1,0:T(1,128)} %counts_ref.1) | copy-start | bytes 772
  4.3 12.8 %collective-permute-start = (bf16[1568,128]{1,0:T(8,128)(2,1)S(1)}, bf16[1568,128]{1,0:T(8,128)(2,1)S(1)}, u32[]{:S(2)}, u32[]{:S(2)}) collective-permute-start(bf16[1568,128]{1,0:T(8,128)(2,1)S(1)} %all_gather.3.both_ref.unused_ref), channel_id=1, source_target_pairs={{0,504},{8,16},{16,8},{24,32},{32,24},{40,48},{48,40},{56,64},{64,... | collective-permute-start | bytes 1204232 | tf_op jit(solution)/shard_map/ppermute | solution.py:200
  11.6 12.6 %collective-permute-start.3 = (bf16[192,1024]{1,0:T(8,128)(2,1)S(1)}, bf16[192,1024]{1,0:T(8,128)(2,1)S(1)}, u32[]{:S(2)}, u32[]{:S(2)}) collective-permute-start(bf16[192,1024]{1,0:T(8,128)(2,1)S(1)} %totals.1.own_ref), channel_id=1, source_target_pairs={{1,0},{2,1},{3,2},{4,3},{5,4},{6,5},{7,6},{9,8},{10,9},{11,10},{12... | collective-permute-start | bytes 1179656 | tf_op jit(solution)/shard_map/ppermute | solution.py:236
  13.6 10.6 %collective-permute-start.1 = (bf16[784,128]{1,0:T(8,128)(2,1)S(1)}, bf16[784,128]{1,0:T(8,128)(2,1)S(1)}, u32[]{:S(2)}, u32[]{:S(2)}) collective-permute-start(bf16[784,128]{1,0:T(8,128)(2,1)S(1)} %touch.1), channel_id=1, source_target_pairs={{0,488},{8,32},{16,504},{24,48},{32,8},{40,64},{48,24},{56,80},{64... | collective-permute-start | bytes 602120 | tf_op jit(solution)/shard_map/ppermute | solution.py:200
  16.9 2.1 %copy-start.2 = (s32[32,24]{0,1:T(8,128)S(1)}, s32[32,24]{0,1:T(8,128)}, u32[]{:S(2)}) copy-start(s32[32,24]{0,1:T(8,128)} %param.9) | copy-start | bytes 9220
  17.1 7.1 %collective-permute-start.2 = (bf16[1568,128]{1,0:T(8,128)(2,1)S(1)}, bf16[1568,128]{1,0:T(8,128)(2,1)S(1)}, u32[]{:S(2)}, u32[]{:S(2)}) collective-permute-start(bf16[1568,128]{1,0:T(8,128)(2,1)S(1)} %collective-permute-done.side_ref), channel_id=1, source_target_pairs={{0,8},{8,0},{16,24},{24,16},{32,40},{40,32},{48,56},{56,48},{64,72... | collective-permute-start | bytes 1204232 | tf_op jit(solution)/shard_map/ppermute | solution.py:200
  26.7 16.9 %all-to-all-start = ((f32[8,4,128]{2,1,0:T(4,128)}), f32[8,4,128]{2,1,0:T(4,128)S(1)}, u32[]{:S(2)}, u32[]{:S(2)}) async-start(f32[8,4,128]{2,1,0:T(4,128)} %sums.1), calls=%async_computation | async-start | bytes 32768 | tf_op jit(solution)/shard_map/all_to_all | solution.py:271

commit v4 on v3

--- a/solution.py
+++ b/solution.py
@@ -8,6 +8,7 @@
 BLK = 2
 LAGS = 1024
 REACH = 3
+BLOCKS = 32
 LANE = 128
 TILE = 128
 VMEM_BYTES = 32 * 1024 * 1024
@@ -60,8 +61,29 @@
     pack_ref[base : base + 16, :] = meta.astype(jnp.bfloat16)
 
 
-def touch_kernel(a_ref, unused_ref, b_ref):
-    b_ref[...] = a_ref[...]
+def select_kernel(odd_ref, pack_ref, unused_ref, far_ref):
+    blocks = BLOCKS
+    rows = 3 * blocks
+    tiles = (pack_ref.shape[0] - 16) // rows
+    slot_row = lax.broadcasted_iota(jnp.int32, (16, LANE), 0)
+    meta = pack_ref[rows * tiles : rows * tiles + 16, :].astype(jnp.float32)
+    slot = jnp.where(odd_ref[0] == 1, 2 * REACH - 1, 0)
+    listed = jnp.sum(jnp.where(slot_row == slot, meta, 0.0), axis=0, keepdims=True)
+    number = lax.broadcasted_iota(jnp.int32, (blocks, blocks), 0).astype(jnp.float32)
+    select = (listed[:, :blocks] == number).astype(jnp.bfloat16)
+    capacity = far_ref.shape[0] // (3 * tiles)
+    for c in range(3):
+        for j in range(0, tiles, 2):
+            pieces = [pack_ref[jj * rows + c * blocks : jj * rows + (c + 1) * blocks, :] for jj in (j, j + 1)]
+            chosen = lax.dot_general(
+                select,
+                jnp.concatenate(pieces, axis=1),
+                (((0,), (0,)), ((), ())),
+                preferred_element_type=jnp.float32,
+            )
+            stack = jnp.concatenate([chosen[:capacity, :LANE], chosen[:capacity, LANE:]], axis=0)
+            at = (c * tiles + j) * capacity
+            far_ref[at : at + 2 * capacity, :] = stack.astype(jnp.bfloat16)
 
 
 def fold(gram):
@@ -143,14 +165,24 @@
     length = own_ref.shape[1]
     base = rows * (length // LANE)
     odd = odd_ref[0] == 1
-    count = far_ref.shape[0]
-    refs = [far_ref, swap_ref.at[pl.ds(0, count)], swap_ref.at[pl.ds(count, count)]]
+    count = base + 16
+    refs = [swap_ref.at[pl.ds(0, count)], swap_ref.at[pl.ds(count, count)]]
     weights = []
-    for ref, at_even, at_odd in zip(refs, (0, 4, 5), (5, 0, 1)):
+    for ref, at_even, at_odd in zip(refs, (4, 5), (0, 1)):
         weights.append(weights_of(jnp.where(odd, at_odd, at_even), ref.at[pl.ds(base, 16)], partners_ref))
+    named = named_by(blocks + jnp.where(odd, 2 * REACH - 1, 0) * slots, partners_ref)[:slots]
+    nothing = jnp.zeros_like(named)
+    first = jnp.concatenate([named, nothing], axis=0).astype(jnp.bfloat16)
+    second = jnp.concatenate([nothing, named], axis=0).astype(jnp.bfloat16)
 
     def store(row, col, field):
-        field_ref[row, col] = (part_ref[row, col] + field).astype(jnp.bfloat16)
+        at = (row.start // blocks * (length // LANE) + col.start // LANE) * slots
+        listed = far_ref[at : at + 2 * slots, :]
+        far = [
+            lax.dot_general(weight, listed, (((0,), (0,)), ((), ())), preferred_element_type=jnp.float32)
+            for weight in (first, second)
+        ]
+        field_ref[row, col] = (part_ref[row, col] + field + jnp.concatenate(far, axis=1)).astype(jnp.bfloat16)
 
     field_terms(jnp.concatenate(weights, axis=0), refs, blocks, length, store)
 
@@ -234,19 +266,19 @@
     own_later = own
     side = moved(both, -1, 1)
     following = lax.ppermute(own_later, "tm", [(i, i - 1) for i in range(1, time_size)])
+    odd = (domain % 2)[None]
     far_pack = pl.pallas_call(
-        touch_kernel,
-        out_shape=jax.ShapeDtypeStruct((pack_rows, LANE), bf16),
-        in_specs=[VMEM, HBM],
+        select_kernel,
+        out_shape=jax.ShapeDtypeStruct((rows // blocks * (length // LANE) * partners.shape[1], LANE), bf16),
+        in_specs=[SMEM, VMEM, HBM],
         out_specs=VMEM,
         compiler_params=PARAMS,
         cost_estimate=pl.CostEstimate(flops=10**6, bytes_accessed=400000, transcendentals=0),
-        name="touch",
-    )(pack, both)
+        name="select",
+    )(odd, pack, both)
     far = moved(far_pack, -3, 3)
     swapped = moved(side, 1, -1)
 
-    odd = (domain % 2)[None]
     side_later = side
     part = pl.pallas_call(
         near_kernel,

time: 44.5 us -> 44.2 us (level)
  waiting for transfers between devices: 11.2 us -> 10.6 us
    ppermute x3, waiting for transfers between devices: 4.79 us -> 4.22 us  [moved(): return lax.ppermute(value, 'space', pairs)]
  transfers between devices with their start and end apart: 5 -> 5, of which waited for: 3 -> 2; matrix products, arithmetic and copies ran while one was open for 0% -> 0% of each run, Pallas kernels for 1% -> 2%
where the time goes in v4:
time: 44.2 us; the launch traced here: 43.9 us
  starting transfers between devices  25 us (57%)
  waiting for transfers between devices  10.6 us (24%)
  Pallas kernels  4.8 us (11%)
  blocking collectives  2.08 us (5%)
  local copies, waits for them, and re-layouts  0.65 us (1%)
  other arithmetic  0.61 us (1%)
    ppermute x3, starting transfers between devices, moved(): return lax.ppermute(value, 'space', pairs)  12.6 us
    all_to_all x1, starting transfers between devices, per_device(): shares = lax.all_to_all(sums, 'tm', 0, 0)  10.5 us
    all_to_all x1, waiting for transfers between devices, per_device(): shares = lax.all_to_all(sums, 'tm', 0, 0)  6.36 us
    ppermute x3, waiting for transfers between devices, moved(): return lax.ppermute(value, 'space', pairs)  4.22 us
    pallas_call x1, Pallas kernels, per_device(): pl.pallas_call(sums_kernel, out_shape=jax.ShapeDtypeStruct((LAGS // LANE,...  2.47 us
    all_gather x1, blocking collectives, per_device(): both = lax.all_gather(pack, 'space', axis_index_groups=pairs, tiled=True)  2.08 us
    ppermute x1, starting transfers between devices, per_device(): lax.ppermute(own_later, 'tm', [(i, i - 1) for i in range(1, time_size)])  1.92 us
    pallas_call x1, Pallas kernels, per_device(): pl.pallas_call(totals_kernel, out_shape=jax.ShapeDtypeStruct((2 * rows, l...  1.41 us
  transfers between devices with their start and end apart: 5, of which 2 were waited for; matrix products, arithmetic and copies ran while one was open for 0% of the time, Pallas kernels for 2%

profile of v4, /device:TPU:64, one launch (start us, length us, event | category | flops | bytes accessed | tf_op | source)
XLA Modules:
  0.0 43.9 jit_solution(5442862775492289499)
XLA Ops:
  0.0 0.0 copy-start
  0.0 1.4 %totals.1.own_ref = bf16[192,1024]{1,0:T(8,128)(2,1)S(1)} custom-call(bf16[3,64,1024]{2,1,0:T(8,128)(2,1)} %bitcast.13, bf16[3,64,1024]{2,1,0:T(8,128)(2,1)} %bitcast.14), custom_call_target="tpu_custom_call" | custom-call | flops 25165824 | bytes 1200000 | tf_op jit(solution)/shard_map/totals/pallas_call | solution.py:234
  1.4 0.0 copy-start.1
  1.4 0.0 copy-done
  1.4 0.6 %copy-done.1 = s32[1,64]{1,0:T(1,128)S(1)} copy-done((s32[1,64]{1,0:T(1,128)S(1)}, s32[1,64]{1,0:T(1,128)}, u32[]{:S(2)}) %copy-start.1) | copy-done | bytes 280
  2.1 0.1 pack.1.pack_ref
  2.2 2.1 %all_gather.3.both_ref.unused_ref = bf16[1568,128]{1,0:T(8,128)(2,1)S(1)} all-gather(bf16[784,128]{1,0:T(8,128)(2,1)S(1)} %pack.1.pack_ref), channel_id=1, replica_groups={{0,8},{16,24},{32,40},{48,56},{64,72},{80,88},{96,104},{112,120},{128,1..., dimensions={0}, use_global_device_ids=true | all-gather | bytes 602112 | tf_op jit(solution)/shard_map/all_gather | solution.py:265
  4.3 7.3 %collective-permute-start = (bf16[1568,128]{1,0:T(8,128)(2,1)S(1)}, bf16[1568,128]{1,0:T(8,128)(2,1)S(1)}, u32[]{:S(2)}, u32[]{:S(2)}) collective-permute-start(bf16[1568,128]{1,0:T(8,128)(2,1)S(1)} %all_gather.3.both_ref.unused_ref), channel_id=1, source_target_pairs={{0,504},{8,16},{16,8},{24,32},{32,24},{40,48},{48,40},{56,64},{64,... | collective-permute-start | bytes 1204232 | tf_op jit(solution)/shard_map/ppermute | solution.py:232
  11.6 1.9 %collective-permute-start.3 = (bf16[192,1024]{1,0:T(8,128)(2,1)S(1)}, bf16[192,1024]{1,0:T(8,128)(2,1)S(1)}, u32[]{:S(2)}, u32[]{:S(2)}) collective-permute-start(bf16[192,1024]{1,0:T(8,128)(2,1)S(1)} %totals.1.own_ref), channel_id=1, source_target_pairs={{1,0},{2,1},{3,2},{4,3},{5,4},{6,5},{7,6},{9,8},{10,9},{11,10},{12... | collective-permute-start | bytes 1179656 | tf_op jit(solution)/shard_map/ppermute | solution.py:268
  13.5 0.0 copy-start.2
  13.6 0.2 select.3
  13.8 3.4 %collective-permute-start.1 = (bf16[576,128]{1,0:T(8,128)(2,1)S(1)}, bf16[576,128]{1,0:T(8,128)(2,1)S(1)}, u32[]{:S(2)}, u32[]{:S(2)}) collective-permute-start(bf16[576,128]{1,0:T(8,128)(2,1)S(1)} %select.3), channel_id=1, source_target_pairs={{0,488},{8,32},{16,504},{24,48},{32,8},{40,64},{48,24},{56,80},{64... | collective-permute-start | bytes 442376 | tf_op jit(solution)/shard_map/ppermute | solution.py:232
  17.2 0.0 collective-permute-done.side_ref
  17.2 1.9 %collective-permute-start.2 = (bf16[1568,128]{1,0:T(8,128)(2,1)S(1)}, bf16[1568,128]{1,0:T(8,128)(2,1)S(1)}, u32[]{:S(2)}, u32[]{:S(2)}) collective-permute-start(bf16[1568,128]{1,0:T(8,128)(2,1)S(1)} %collective-permute-done.side_ref), channel_id=1, source_target_pairs={{0,8},{8,0},{16,24},{24,16},{32,40},{40,32},{48,56},{56,48},{64,72... | collective-permute-start | bytes 1204232 | tf_op jit(solution)/shard_map/ppermute | solution.py:232
  19.1 0.0 copy-done.2
  19.1 0.5 %near.1.part_ref = f32[96,1024]{1,0:T(8,128)S(1)} custom-call(s32[1]{0:T(128)} %bitcast.odd_ref, s32[24,32]{1,0:T(8,128)S(1)} %bitcast.11, bf16[1568,128]{1,0:T(8,128)(2,1)S(1)} %all_gather.3.both_ref.unused_ref, bf16[1568,128]{1,0:T(8,128)(2,1)S(1)} %collective-permute-done.side_ref), custom_call_target="tpu_custom_call" | custom-call | flops 10000000000 | bytes 1000000 | tf_op jit(solution)/shard_map/near/pallas_call | solution.py:283
  19.7 4.2 %collective-permute-done.1.far_ref = bf16[576,128]{1,0:T(8,128)(2,1)S(1)} collective-permute-done((bf16[576,128]{1,0:T(8,128)(2,1)S(1)}, bf16[576,128]{1,0:T(8,128)(2,1)S(1)}, u32[]{:S(2)}, u32[]{:S(2)}) %collective-permute-start.1) | collective-permute-done | bytes 147488 | tf_op jit(solution)/shard_map/ppermute | solution.py:232
  23.9 0.0 collective-permute-done.3.next_ref
  23.9 0.0 collective-permute-done.2.swap_ref
  23.9 2.5 %sums.1 = f32[8,4,128]{2,1,0:T(4,128)} custom-call(s32[1]{0:T(128)} %bitcast.odd_ref, s32[24,32]{1,0:T(8,128)S(1)} %bitcast.12, f32[96,1024]{1,0:T(8,128)S(1)} %near.1.part_ref, bf16[576,128]{1,0:T(8,128)(2,1)S(1)} %collective-permute-done.1.far_ref, bf16[1568,128]{1,0:T(8,128)(2,1)S(1)} %collective-permute-done.2.swap_ref, ...), custom_call_target="tpu_custom_call" | custom-call | flops 600000000 | bytes 2500000 | tf_op jit(solution)/shard_map/sums/pallas_call | solution.py:292
  26.4 10.5 %all-to-all-start = ((f32[8,4,128]{2,1,0:T(4,128)}), f32[8,4,128]{2,1,0:T(4,128)S(1)}, u32[]{:S(2)}, u32[]{:S(2)}) async-start(f32[8,4,128]{2,1,0:T(4,128)} %sums.1), calls=%async_computation | async-start | bytes 32768 | tf_op jit(solution)/shard_map/all_to_all | solution.py:303
  36.9 6.4 %all-to-all-done = f32[8,4,128]{2,1,0:T(4,128)S(1)} async-done(((f32[8,4,128]{2,1,0:T(4,128)}), f32[8,4,128]{2,1,0:T(4,128)S(1)}, u32[]{:S(2)}, u32[]{:S(2)}) %all-to-all-start) | async-done | bytes 16416 | tf_op jit(solution)/shard_map/all_to_all | solution.py:303
  43.3 0.6 %bitcast_divide_fusion = f32[1,4,128]{2,1,0:T(4,128)} fusion(f32[4,128]{1,0:T(4,128)S(1)} %reduce_sum.11, f32[128]{0:T(128)S(1)} %subtract_convert_fusion), kind=kLoop, calls=%fused_computation | loop fusion | flops 512 | bytes 4608 | tf_op jit(solution)/shard_map/div | solution.py:307
  (2 shorter events, 0.0 us)
Async XLA Ops:
  0.0 1.4 %copy-start = (s32[1,64,24]{1,2,0:T(8,128)S(1)}, s32[1,64,24]{1,2,0:T(8,128)}, u32[]{:S(2)}) copy-start(s32[1,64,24]{1,2,0:T(8,128)} %param.8) | copy-start | bytes 18436
  1.4 0.7 %copy-start.1 = (s32[1,64]{1,0:T(1,128)S(1)}, s32[1,64]{1,0:T(1,128)}, u32[]{:S(2)}) copy-start(s32[1,64]{1,0:T(1,128)} %counts_ref.1) | copy-start | bytes 772
  4.3 12.9 %collective-permute-start = (bf16[1568,128]{1,0:T(8,128)(2,1)S(1)}, bf16[1568,128]{1,0:T(8,128)(2,1)S(1)}, u32[]{:S(2)}, u32[]{:S(2)}) collective-permute-start(bf16[1568,128]{1,0:T(8,128)(2,1)S(1)} %all_gather.3.both_ref.unused_ref), channel_id=1, source_target_pairs={{0,504},{8,16},{16,8},{24,32},{32,24},{40,48},{48,40},{56,64},{64,... | collective-permute-start | bytes 1204232 | tf_op jit(solution)/shard_map/ppermute | solution.py:232
  11.6 12.3 %collective-permute-start.3 = (bf16[192,1024]{1,0:T(8,128)(2,1)S(1)}, bf16[192,1024]{1,0:T(8,128)(2,1)S(1)}, u32[]{:S(2)}, u32[]{:S(2)}) collective-permute-start(bf16[192,1024]{1,0:T(8,128)(2,1)S(1)} %totals.1.own_ref), channel_id=1, source_target_pairs={{1,0},{2,1},{3,2},{4,3},{5,4},{6,5},{7,6},{9,8},{10,9},{11,10},{12... | collective-permute-start | bytes 1179656 | tf_op jit(solution)/shard_map/ppermute | solution.py:268
  13.5 5.6 %copy-start.2 = (s32[32,24]{0,1:T(8,128)S(1)}, s32[32,24]{0,1:T(8,128)}, u32[]{:S(2)}) copy-start(s32[32,24]{0,1:T(8,128)} %param.9) | copy-start | bytes 9220
  13.8 10.1 %collective-permute-start.1 = (bf16[576,128]{1,0:T(8,128)(2,1)S(1)}, bf16[576,128]{1,0:T(8,128)(2,1)S(1)}, u32[]{:S(2)}, u32[]{:S(2)}) collective-permute-start(bf16[576,128]{1,0:T(8,128)(2,1)S(1)} %select.3), channel_id=1, source_target_pairs={{0,488},{8,32},{16,504},{24,48},{32,8},{40,64},{48,24},{56,80},{64... | collective-permute-start | bytes 442376 | tf_op jit(solution)/shard_map/ppermute | solution.py:232
  17.2 6.7 %collective-permute-start.2 = (bf16[1568,128]{1,0:T(8,128)(2,1)S(1)}, bf16[1568,128]{1,0:T(8,128)(2,1)S(1)}, u32[]{:S(2)}, u32[]{:S(2)}) collective-permute-start(bf16[1568,128]{1,0:T(8,128)(2,1)S(1)} %collective-permute-done.side_ref), channel_id=1, source_target_pairs={{0,8},{8,0},{16,24},{24,16},{32,40},{40,32},{48,56},{56,48},{64,72... | collective-permute-start | bytes 1204232 | tf_op jit(solution)/shard_map/ppermute | solution.py:232
  26.4 16.9 %all-to-all-start = ((f32[8,4,128]{2,1,0:T(4,128)}), f32[8,4,128]{2,1,0:T(4,128)S(1)}, u32[]{:S(2)}, u32[]{:S(2)}) async-start(f32[8,4,128]{2,1,0:T(4,128)} %sums.1), calls=%async_computation | async-start | bytes 32768 | tf_op jit(solution)/shard_map/all_to_all | solution.py:303

commit v5 on v4

--- a/solution.py
+++ b/solution.py
@@ -1,3 +1,5 @@
+import functools
+
 import jax
 import jax.numpy as jnp
 from jax import lax
@@ -159,7 +161,7 @@
     field_terms(jnp.concatenate(weights, axis=0), refs, blocks, length, store)
 
 
-def sums_kernel(odd_ref, partners_ref, part_ref, far_ref, swap_ref, own_ref, next_ref, out_ref, field_ref):
+def sums_kernel(steps_in_all, odd_ref, partners_ref, part_ref, far_ref, swap_ref, own_ref, next_ref, out_ref, field_ref):
     slots, blocks = partners_ref.shape
     rows = 3 * blocks
     length = own_ref.shape[1]
@@ -207,7 +209,9 @@
         else:
             sums = fold(gram(2 * blocks, rows + (q - 1) * blocks, blocks))
         for j in range(LAGS // LANE):
-            out_ref[j, q : q + 1, :] = sums[:, j * LANE : (j + 1) * LANE]
+            lag = lax.broadcasted_iota(jnp.int32, (1, LANE), 1) + j * LANE
+            anchors = (steps_in_all - lag).astype(jnp.float32)
+            out_ref[j, q : q + 1, :] = sums[:, j * LANE : (j + 1) * LANE] / anchors
 
 
 VMEM = pl.BlockSpec(memory_space=pltpu.VMEM)
@@ -290,7 +294,7 @@
         name="near",
     )(odd, partners.T, both, side_later)
     sums = pl.pallas_call(
-        sums_kernel,
+        functools.partial(sums_kernel, length * time_size),
         out_shape=jax.ShapeDtypeStruct((LAGS // LANE, 4, LANE), jnp.float32),
         in_specs=[SMEM] + [VMEM] * 6,
         out_specs=VMEM,
@@ -301,10 +305,7 @@
     )(odd, partners.T, part, far, swapped, own, following)
 
     shares = lax.all_to_all(sums, "tm", 0, 0)
-    lag_share = LAGS // time_size
-    lag_index = lax.axis_index("tm") * lag_share + jnp.arange(lag_share, dtype=jnp.int32)
-    anchor_count = (length * time_size - lag_index).astype(jnp.float32)
-    return (jnp.sum(shares, axis=0) / anchor_count[None, :])[None]
+    return jnp.sum(shares, axis=0)[None]
 
 
 def solution(mesh):

time: 44.2 us -> 43.3 us (0.980)
  blocking collectives: 2.08 us -> 18.8 us
  starting transfers between devices: 25 us -> 14.5 us
  waiting for transfers between devices: 10.6 us -> 4.23 us
  Pallas kernels: 4.8 us -> 4.19 us
    all_to_all x0 -> x1, blocking collectives: none -> 16.7 us  [per_device(): shares = lax.all_to_all(sums, 'tm', 0, 0)]
    all_to_all x1 -> x0, starting transfers between devices: 10.5 us -> none  [per_device(): shares = lax.all_to_all(sums, 'tm', 0, 0)]
    all_to_all x1 -> x0, waiting for transfers between devices: 6.36 us -> none  [per_device(): shares = lax.all_to_all(sums, 'tm', 0, 0)]
    pallas_call x1, Pallas kernels: 2.47 us -> 1.87 us  [per_device(): pl.pallas_call(functools.partial(sums_kernel, length * time_size), out_sh...]
    div x1 -> x0, other arithmetic: 0.59 us -> none  [per_device(): return (jnp.sum(shares, axis=0) / anchor_count[None, :])[None]]
    reduce_sum x1, other arithmetic: 0.02 us -> 0.59 us  [per_device(): return jnp.sum(shares, axis=0)[None]]
  transfers between devices with their start and end apart: 5 -> 4, of which waited for: 2 -> 1; matrix products, arithmetic and copies ran while one was open for 0% -> 0% of each run, Pallas kernels for 2% -> 2%
where the time goes in v5:
time: 43.3 us; the launch traced here: 43 us
  blocking collectives  18.8 us (43%)
  starting transfers between devices  14.5 us (33%)
  waiting for transfers between devices  4.23 us (10%)
  Pallas kernels  4.19 us (10%)
  local copies, waits for them, and re-layouts  0.65 us (2%)
  other arithmetic  0.59 us (1%)
    all_to_all x1, blocking collectives, per_device(): shares = lax.all_to_all(sums, 'tm', 0, 0)  16.7 us
    ppermute x3, starting transfers between devices, moved(): return lax.ppermute(value, 'space', pairs)  12.6 us
    ppermute x3, waiting for transfers between devices, moved(): return lax.ppermute(value, 'space', pairs)  4.22 us
    all_gather x1, blocking collectives, per_device(): both = lax.all_gather(pack, 'space', axis_index_groups=pairs, tiled=True)  2.08 us
    ppermute x1, starting transfers between devices, per_device(): lax.ppermute(own_later, 'tm', [(i, i - 1) for i in range(1, time_size)])  1.92 us
    pallas_call x1, Pallas kernels, per_device(): pl.pallas_call(functools.partial(sums_kernel, length * time_size), out_sh...  1.87 us
    pallas_call x1, Pallas kernels, per_device(): pl.pallas_call(totals_kernel, out_shape=jax.ShapeDtypeStruct((2 * rows, l...  1.41 us
  transfers between devices with their start and end apart: 4, of which 1 were waited for; matrix products, arithmetic and copies ran while one was open for 0% of the time, Pallas kernels for 2%

profile of v5, /device:TPU:64, one launch (start us, length us, event | category | flops | bytes accessed | tf_op | source)
XLA Modules:
  0.0 43.0 jit_solution(17427835188692826601)
XLA Ops:
  0.0 0.0 copy-start
  0.0 1.4 %totals.1.own_ref = bf16[192,1024]{1,0:T(8,128)(2,1)S(1)} custom-call(bf16[3,64,1024]{2,1,0:T(8,128)(2,1)} %bitcast.12, bf16[3,64,1024]{2,1,0:T(8,128)(2,1)} %bitcast.13), custom_call_target="tpu_custom_call" | custom-call | flops 25165824 | bytes 1200000 | tf_op jit(solution)/shard_map/totals/pallas_call | solution.py:238
  1.4 0.0 copy-start.1
  1.4 0.0 copy-done
  1.4 0.6 %copy-done.1 = s32[1,64]{1,0:T(1,128)S(1)} copy-done((s32[1,64]{1,0:T(1,128)S(1)}, s32[1,64]{1,0:T(1,128)}, u32[]{:S(2)}) %copy-start.1) | copy-done | bytes 280
  2.1 0.1 pack.1.pack_ref
  2.2 2.1 %all_gather.3.both_ref.unused_ref = bf16[1568,128]{1,0:T(8,128)(2,1)S(1)} all-gather(bf16[784,128]{1,0:T(8,128)(2,1)S(1)} %pack.1.pack_ref), channel_id=1, replica_groups={{0,8},{16,24},{32,40},{48,56},{64,72},{80,88},{96,104},{112,120},{128,1..., dimensions={0}, use_global_device_ids=true | all-gather | bytes 602112 | tf_op jit(solution)/shard_map/all_gather | solution.py:269
  4.3 7.3 %collective-permute-start = (bf16[1568,128]{1,0:T(8,128)(2,1)S(1)}, bf16[1568,128]{1,0:T(8,128)(2,1)S(1)}, u32[]{:S(2)}, u32[]{:S(2)}) collective-permute-start(bf16[1568,128]{1,0:T(8,128)(2,1)S(1)} %all_gather.3.both_ref.unused_ref), channel_id=1, source_target_pairs={{0,504},{8,16},{16,8},{24,32},{32,24},{40,48},{48,40},{56,64},{64,... | collective-permute-start | bytes 1204232 | tf_op jit(solution)/shard_map/ppermute | solution.py:236
  11.6 1.9 %collective-permute-start.3 = (bf16[192,1024]{1,0:T(8,128)(2,1)S(1)}, bf16[192,1024]{1,0:T(8,128)(2,1)S(1)}, u32[]{:S(2)}, u32[]{:S(2)}) collective-permute-start(bf16[192,1024]{1,0:T(8,128)(2,1)S(1)} %totals.1.own_ref), channel_id=1, source_target_pairs={{1,0},{2,1},{3,2},{4,3},{5,4},{6,5},{7,6},{9,8},{10,9},{11,10},{12... | collective-permute-start | bytes 1179656 | tf_op jit(solution)/shard_map/ppermute | solution.py:272
  13.5 0.0 copy-start.2
  13.6 0.2 select.3
  13.8 3.4 %collective-permute-start.1 = (bf16[576,128]{1,0:T(8,128)(2,1)S(1)}, bf16[576,128]{1,0:T(8,128)(2,1)S(1)}, u32[]{:S(2)}, u32[]{:S(2)}) collective-permute-start(bf16[576,128]{1,0:T(8,128)(2,1)S(1)} %select.3), channel_id=1, source_target_pairs={{0,488},{8,32},{16,504},{24,48},{32,8},{40,64},{48,24},{56,80},{64... | collective-permute-start | bytes 442376 | tf_op jit(solution)/shard_map/ppermute | solution.py:236
  17.2 0.0 collective-permute-done.side_ref
  17.2 1.9 %collective-permute-start.2 = (bf16[1568,128]{1,0:T(8,128)(2,1)S(1)}, bf16[1568,128]{1,0:T(8,128)(2,1)S(1)}, u32[]{:S(2)}, u32[]{:S(2)}) collective-permute-start(bf16[1568,128]{1,0:T(8,128)(2,1)S(1)} %collective-permute-done.side_ref), channel_id=1, source_target_pairs={{0,8},{8,0},{16,24},{24,16},{32,40},{40,32},{48,56},{56,48},{64,72... | collective-permute-start | bytes 1204232 | tf_op jit(solution)/shard_map/ppermute | solution.py:236
  19.1 0.0 copy-done.2
  19.1 0.5 %near.1.part_ref = f32[96,1024]{1,0:T(8,128)S(1)} custom-call(s32[1]{0:T(128)} %bitcast.odd_ref, s32[24,32]{1,0:T(8,128)S(1)} %bitcast.10, bf16[1568,128]{1,0:T(8,128)(2,1)S(1)} %all_gather.3.both_ref.unused_ref, bf16[1568,128]{1,0:T(8,128)(2,1)S(1)} %collective-permute-done.side_ref), custom_call_target="tpu_custom_call" | custom-call | flops 10000000000 | bytes 1000000 | tf_op jit(solution)/shard_map/near/pallas_call | solution.py:287
  19.7 4.2 %collective-permute-done.1.far_ref = bf16[576,128]{1,0:T(8,128)(2,1)S(1)} collective-permute-done((bf16[576,128]{1,0:T(8,128)(2,1)S(1)}, bf16[576,128]{1,0:T(8,128)(2,1)S(1)}, u32[]{:S(2)}, u32[]{:S(2)}) %collective-permute-start.1) | collective-permute-done | bytes 147488 | tf_op jit(solution)/shard_map/ppermute | solution.py:236
  23.9 0.0 collective-permute-done.3.next_ref
  23.9 0.0 collective-permute-done.2.swap_ref
  23.9 1.9 %sums.1 = f32[8,4,128]{2,1,0:T(4,128)S(1)} custom-call(s32[1]{0:T(128)} %bitcast.odd_ref, s32[24,32]{1,0:T(8,128)S(1)} %bitcast.11, f32[96,1024]{1,0:T(8,128)S(1)} %near.1.part_ref, bf16[576,128]{1,0:T(8,128)(2,1)S(1)} %collective-permute-done.1.far_ref, bf16[1568,128]{1,0:T(8,128)(2,1)S(1)} %collective-permute-done.2.swap_ref, ...), custom_call_target="tpu_custom_call" | custom-call | flops 600000000 | bytes 2500000 | tf_op jit(solution)/shard_map/sums/pallas_call | solution.py:296
  25.8 16.7 %all_to_all.5 = f32[8,4,128]{2,1,0:T(4,128)S(1)} all-to-all(f32[8,4,128]{2,1,0:T(4,128)S(1)} %sums.1), channel_id=1, replica_groups=mesh['space'=64,'tm'=8] {'tm'}, dimensions={0} | all-to-all | bytes 32768 | tf_op jit(solution)/shard_map/all_to_all | solution.py:307
  42.4 0.6 %reduce_sum.9 = f32[4,128]{1,0:T(4,128)} reduce(f32[8,4,128]{2,1,0:T(4,128)S(1)} %all_to_all.5, f32[]{:T(128)} %constant.20.clone.1), dimensions={0}, to_apply=%region_0.1 | reduce | flops 3584 | bytes 18436 | tf_op jit(solution)/shard_map/reduce_sum | solution.py:308
Async XLA Ops:
  0.0 1.4 %copy-start = (s32[1,64,24]{1,2,0:T(8,128)S(1)}, s32[1,64,24]{1,2,0:T(8,128)}, u32[]{:S(2)}) copy-start(s32[1,64,24]{1,2,0:T(8,128)} %param.8) | copy-start | bytes 18436
  1.4 0.7 %copy-start.1 = (s32[1,64]{1,0:T(1,128)S(1)}, s32[1,64]{1,0:T(1,128)}, u32[]{:S(2)}) copy-start(s32[1,64]{1,0:T(1,128)} %counts_ref.1) | copy-start | bytes 772
  4.3 12.9 %collective-permute-start = (bf16[1568,128]{1,0:T(8,128)(2,1)S(1)}, bf16[1568,128]{1,0:T(8,128)(2,1)S(1)}, u32[]{:S(2)}, u32[]{:S(2)}) collective-permute-start(bf16[1568,128]{1,0:T(8,128)(2,1)S(1)} %all_gather.3.both_ref.unused_ref), channel_id=1, source_target_pairs={{0,504},{8,16},{16,8},{24,32},{32,24},{40,48},{48,40},{56,64},{64,... | collective-permute-start | bytes 1204232 | tf_op jit(solution)/shard_map/ppermute | solution.py:236
  11.6 12.3 %collective-permute-start.3 = (bf16[192,1024]{1,0:T(8,128)(2,1)S(1)}, bf16[192,1024]{1,0:T(8,128)(2,1)S(1)}, u32[]{:S(2)}, u32[]{:S(2)}) collective-permute-start(bf16[192,1024]{1,0:T(8,128)(2,1)S(1)} %totals.1.own_ref), channel_id=1, source_target_pairs={{1,0},{2,1},{3,2},{4,3},{5,4},{6,5},{7,6},{9,8},{10,9},{11,10},{12... | collective-permute-start | bytes 1179656 | tf_op jit(solution)/shard_map/ppermute | solution.py:272
  13.5 5.6 %copy-start.2 = (s32[32,24]{0,1:T(8,128)S(1)}, s32[32,24]{0,1:T(8,128)}, u32[]{:S(2)}) copy-start(s32[32,24]{0,1:T(8,128)} %param.9) | copy-start | bytes 9220
  13.8 10.1 %collective-permute-start.1 = (bf16[576,128]{1,0:T(8,128)(2,1)S(1)}, bf16[576,128]{1,0:T(8,128)(2,1)S(1)}, u32[]{:S(2)}, u32[]{:S(2)}) collective-permute-start(bf16[576,128]{1,0:T(8,128)(2,1)S(1)} %select.3), channel_id=1, source_target_pairs={{0,488},{8,32},{16,504},{24,48},{32,8},{40,64},{48,24},{56,80},{64... | collective-permute-start | bytes 442376 | tf_op jit(solution)/shard_map/ppermute | solution.py:236
  17.2 6.7 %collective-permute-start.2 = (bf16[1568,128]{1,0:T(8,128)(2,1)S(1)}, bf16[1568,128]{1,0:T(8,128)(2,1)S(1)}, u32[]{:S(2)}, u32[]{:S(2)}) collective-permute-start(bf16[1568,128]{1,0:T(8,128)(2,1)S(1)} %collective-permute-done.side_ref), channel_id=1, source_target_pairs={{0,8},{8,0},{16,24},{24,16},{32,40},{40,32},{48,56},{56,48},{64,72... | collective-permute-start | bytes 1204232 | tf_op jit(solution)/shard_map/ppermute | solution.py:236

commit v6 on v5

--- a/solution.py
+++ b/solution.py
@@ -188,26 +188,25 @@
 
     field_terms(jnp.concatenate(weights, axis=0), refs, blocks, length, store)
 
-    span = TILE + LAGS
-    steps = length // TILE
-
-    def later(first, count, i):
-        lo = i * TILE
+    def later(first, count, i, tile):
+        lo = i * tile
+        span = tile + LAGS
         here = own_ref[first : first + count, lo:length]
         return jnp.concatenate([here, next_ref[first : first + count, 0 : span - (length - lo)]], axis=1)
 
-    def gram(anchor_first, window_first, count):
+    def gram(anchor_first, window_first, count, tile):
+        steps = length // tile
         anchors = jnp.concatenate(
-            [field_ref[anchor_first : anchor_first + count, i * TILE : (i + 1) * TILE] for i in range(steps)], axis=0
+            [field_ref[anchor_first : anchor_first + count, i * tile : (i + 1) * tile] for i in range(steps)], axis=0
         )
-        window = jnp.concatenate([later(window_first, count, i) for i in range(steps)], axis=0)
+        window = jnp.concatenate([later(window_first, count, i, tile) for i in range(steps)], axis=0)
         return lax.dot_general(anchors, window, (((0,), (0,)), ((), ())), preferred_element_type=jnp.float32)
 
     for q in range(4):
         if q == 0:
-            sums = fold(gram(0, 0, rows))
+            sums = fold(gram(0, 0, rows, 2 * TILE))
         else:
-            sums = fold(gram(2 * blocks, rows + (q - 1) * blocks, blocks))
+            sums = fold(gram(2 * blocks, rows + (q - 1) * blocks, blocks, TILE))
         for j in range(LAGS // LANE):
             lag = lax.broadcasted_iota(jnp.int32, (1, LANE), 1) + j * LANE
             anchors = (steps_in_all - lag).astype(jnp.float32)

time: 43.3 us -> 43.4 us (level)
  no operation moved by 1% of the time
where the time goes in v6:
time: 43.4 us; the launch traced here: 43.1 us
  blocking collectives  18.8 us (43%)
  starting transfers between devices  14.5 us (33%)
  Pallas kernels  4.24 us (10%)
  waiting for transfers between devices  4.23 us (10%)
  local copies, waits for them, and re-layouts  0.65 us (1%)
  other arithmetic  0.59 us (1%)
    all_to_all x1, blocking collectives, per_device(): shares = lax.all_to_all(sums, 'tm', 0, 0)  16.7 us
    ppermute x3, starting transfers between devices, moved(): return lax.ppermute(value, 'space', pairs)  12.6 us
    ppermute x3, waiting for transfers between devices, moved(): return lax.ppermute(value, 'space', pairs)  4.22 us
    all_gather x1, blocking collectives, per_device(): both = lax.all_gather(pack, 'space', axis_index_groups=pairs, tiled=True)  2.08 us
    ppermute x1, starting transfers between devices, per_device(): lax.ppermute(own_later, 'tm', [(i, i - 1) for i in range(1, time_size)])  1.92 us
    pallas_call x1, Pallas kernels, per_device(): pl.pallas_call(functools.partial(sums_kernel, length * time_size), out_sh...  1.92 us
    pallas_call x1, Pallas kernels, per_device(): pl.pallas_call(totals_kernel, out_shape=jax.ShapeDtypeStruct((2 * rows, l...  1.41 us
  transfers between devices with their start and end apart: 4, of which 1 were waited for; matrix products, arithmetic and copies ran while one was open for 0% of the time, Pallas kernels for 2%

profile of v6, /device:TPU:64, one launch (start us, length us, event | category | flops | bytes accessed | tf_op | source)
XLA Modules:
  0.0 43.1 jit_solution(17593254463418885905)
XLA Ops:
  0.0 0.0 copy-start
  0.0 1.4 %totals.1.own_ref = bf16[192,1024]{1,0:T(8,128)(2,1)S(1)} custom-call(bf16[3,64,1024]{2,1,0:T(8,128)(2,1)} %bitcast.12, bf16[3,64,1024]{2,1,0:T(8,128)(2,1)} %bitcast.13), custom_call_target="tpu_custom_call" | custom-call | flops 25165824 | bytes 1200000 | tf_op jit(solution)/shard_map/totals/pallas_call | solution.py:237
  1.4 0.0 copy-start.1
  1.4 0.0 copy-done
  1.4 0.6 %copy-done.1 = s32[1,64]{1,0:T(1,128)S(1)} copy-done((s32[1,64]{1,0:T(1,128)S(1)}, s32[1,64]{1,0:T(1,128)}, u32[]{:S(2)}) %copy-start.1) | copy-done | bytes 280
  2.1 0.1 pack.1.pack_ref
  2.2 2.1 %all_gather.3.both_ref.unused_ref = bf16[1568,128]{1,0:T(8,128)(2,1)S(1)} all-gather(bf16[784,128]{1,0:T(8,128)(2,1)S(1)} %pack.1.pack_ref), channel_id=1, replica_groups={{0,8},{16,24},{32,40},{48,56},{64,72},{80,88},{96,104},{112,120},{128,1..., dimensions={0}, use_global_device_ids=true | all-gather | bytes 602112 | tf_op jit(solution)/shard_map/all_gather | solution.py:268
  4.3 7.3 %collective-permute-start = (bf16[1568,128]{1,0:T(8,128)(2,1)S(1)}, bf16[1568,128]{1,0:T(8,128)(2,1)S(1)}, u32[]{:S(2)}, u32[]{:S(2)}) collective-permute-start(bf16[1568,128]{1,0:T(8,128)(2,1)S(1)} %all_gather.3.both_ref.unused_ref), channel_id=1, source_target_pairs={{0,504},{8,16},{16,8},{24,32},{32,24},{40,48},{48,40},{56,64},{64,... | collective-permute-start | bytes 1204232 | tf_op jit(solution)/shard_map/ppermute | solution.py:235
  11.6 1.9 %collective-permute-start.3 = (bf16[192,1024]{1,0:T(8,128)(2,1)S(1)}, bf16[192,1024]{1,0:T(8,128)(2,1)S(1)}, u32[]{:S(2)}, u32[]{:S(2)}) collective-permute-start(bf16[192,1024]{1,0:T(8,128)(2,1)S(1)} %totals.1.own_ref), channel_id=1, source_target_pairs={{1,0},{2,1},{3,2},{4,3},{5,4},{6,5},{7,6},{9,8},{10,9},{11,10},{12... | collective-permute-start | bytes 1179656 | tf_op jit(solution)/shard_map/ppermute | solution.py:271
  13.5 0.0 copy-start.2
  13.6 0.2 select.3
  13.8 3.4 %collective-permute-start.1 = (bf16[576,128]{1,0:T(8,128)(2,1)S(1)}, bf16[576,128]{1,0:T(8,128)(2,1)S(1)}, u32[]{:S(2)}, u32[]{:S(2)}) collective-permute-start(bf16[576,128]{1,0:T(8,128)(2,1)S(1)} %select.3), channel_id=1, source_target_pairs={{0,488},{8,32},{16,504},{24,48},{32,8},{40,64},{48,24},{56,80},{64... | collective-permute-start | bytes 442376 | tf_op jit(solution)/shard_map/ppermute | solution.py:235
  17.2 0.0 collective-permute-done.side_ref
  17.2 1.9 %collective-permute-start.2 = (bf16[1568,128]{1,0:T(8,128)(2,1)S(1)}, bf16[1568,128]{1,0:T(8,128)(2,1)S(1)}, u32[]{:S(2)}, u32[]{:S(2)}) collective-permute-start(bf16[1568,128]{1,0:T(8,128)(2,1)S(1)} %collective-permute-done.side_ref), channel_id=1, source_target_pairs={{0,8},{8,0},{16,24},{24,16},{32,40},{40,32},{48,56},{56,48},{64,72... | collective-permute-start | bytes 1204232 | tf_op jit(solution)/shard_map/ppermute | solution.py:235
  19.1 0.0 copy-done.2
  19.1 0.5 %near.1.part_ref = f32[96,1024]{1,0:T(8,128)S(1)} custom-call(s32[1]{0:T(128)} %bitcast.odd_ref, s32[24,32]{1,0:T(8,128)S(1)} %bitcast.10, bf16[1568,128]{1,0:T(8,128)(2,1)S(1)} %all_gather.3.both_ref.unused_ref, bf16[1568,128]{1,0:T(8,128)(2,1)S(1)} %collective-permute-done.side_ref), custom_call_target="tpu_custom_call" | custom-call | flops 10000000000 | bytes 1000000 | tf_op jit(solution)/shard_map/near/pallas_call | solution.py:286
  19.7 4.2 %collective-permute-done.1.far_ref = bf16[576,128]{1,0:T(8,128)(2,1)S(1)} collective-permute-done((bf16[576,128]{1,0:T(8,128)(2,1)S(1)}, bf16[576,128]{1,0:T(8,128)(2,1)S(1)}, u32[]{:S(2)}, u32[]{:S(2)}) %collective-permute-start.1) | collective-permute-done | bytes 147488 | tf_op jit(solution)/shard_map/ppermute | solution.py:235
  23.9 0.0 collective-permute-done.3.next_ref
  23.9 0.0 collective-permute-done.2.swap_ref
  23.9 1.9 %sums.1 = f32[8,4,128]{2,1,0:T(4,128)S(1)} custom-call(s32[1]{0:T(128)} %bitcast.odd_ref, s32[24,32]{1,0:T(8,128)S(1)} %bitcast.11, f32[96,1024]{1,0:T(8,128)S(1)} %near.1.part_ref, bf16[576,128]{1,0:T(8,128)(2,1)S(1)} %collective-permute-done.1.far_ref, bf16[1568,128]{1,0:T(8,128)(2,1)S(1)} %collective-permute-done.2.swap_ref, ...), custom_call_target="tpu_custom_call" | custom-call | flops 600000000 | bytes 2500000 | tf_op jit(solution)/shard_map/sums/pallas_call | solution.py:295
  25.8 16.7 %all_to_all.5 = f32[8,4,128]{2,1,0:T(4,128)S(1)} all-to-all(f32[8,4,128]{2,1,0:T(4,128)S(1)} %sums.1), channel_id=1, replica_groups=mesh['space'=64,'tm'=8] {'tm'}, dimensions={0} | all-to-all | bytes 32768 | tf_op jit(solution)/shard_map/all_to_all | solution.py:306
  42.5 0.6 %reduce_sum.9 = f32[4,128]{1,0:T(4,128)} reduce(f32[8,4,128]{2,1,0:T(4,128)S(1)} %all_to_all.5, f32[]{:T(128)} %constant.20.clone.1), dimensions={0}, to_apply=%region_0.1 | reduce | flops 3584 | bytes 18436 | tf_op jit(solution)/shard_map/reduce_sum | solution.py:307
Async XLA Ops:
  0.0 1.4 %copy-start = (s32[1,64,24]{1,2,0:T(8,128)S(1)}, s32[1,64,24]{1,2,0:T(8,128)}, u32[]{:S(2)}) copy-start(s32[1,64,24]{1,2,0:T(8,128)} %param.8) | copy-start | bytes 18436
  1.4 0.7 %copy-start.1 = (s32[1,64]{1,0:T(1,128)S(1)}, s32[1,64]{1,0:T(1,128)}, u32[]{:S(2)}) copy-start(s32[1,64]{1,0:T(1,128)} %counts_ref.1) | copy-start | bytes 772
  4.3 12.9 %collective-permute-start = (bf16[1568,128]{1,0:T(8,128)(2,1)S(1)}, bf16[1568,128]{1,0:T(8,128)(2,1)S(1)}, u32[]{:S(2)}, u32[]{:S(2)}) collective-permute-start(bf16[1568,128]{1,0:T(8,128)(2,1)S(1)} %all_gather.3.both_ref.unused_ref), channel_id=1, source_target_pairs={{0,504},{8,16},{16,8},{24,32},{32,24},{40,48},{48,40},{56,64},{64,... | collective-permute-start | bytes 1204232 | tf_op jit(solution)/shard_map/ppermute | solution.py:235
  11.6 12.3 %collective-permute-start.3 = (bf16[192,1024]{1,0:T(8,128)(2,1)S(1)}, bf16[192,1024]{1,0:T(8,128)(2,1)S(1)}, u32[]{:S(2)}, u32[]{:S(2)}) collective-permute-start(bf16[192,1024]{1,0:T(8,128)(2,1)S(1)} %totals.1.own_ref), channel_id=1, source_target_pairs={{1,0},{2,1},{3,2},{4,3},{5,4},{6,5},{7,6},{9,8},{10,9},{11,10},{12... | collective-permute-start | bytes 1179656 | tf_op jit(solution)/shard_map/ppermute | solution.py:271
  13.5 5.6 %copy-start.2 = (s32[32,24]{0,1:T(8,128)S(1)}, s32[32,24]{0,1:T(8,128)}, u32[]{:S(2)}) copy-start(s32[32,24]{0,1:T(8,128)} %param.9) | copy-start | bytes 9220
  13.8 10.1 %collective-permute-start.1 = (bf16[576,128]{1,0:T(8,128)(2,1)S(1)}, bf16[576,128]{1,0:T(8,128)(2,1)S(1)}, u32[]{:S(2)}, u32[]{:S(2)}) collective-permute-start(bf16[576,128]{1,0:T(8,128)(2,1)S(1)} %select.3), channel_id=1, source_target_pairs={{0,488},{8,32},{16,504},{24,48},{32,8},{40,64},{48,24},{56,80},{64... | collective-permute-start | bytes 442376 | tf_op jit(solution)/shard_map/ppermute | solution.py:235
  17.2 6.7 %collective-permute-start.2 = (bf16[1568,128]{1,0:T(8,128)(2,1)S(1)}, bf16[1568,128]{1,0:T(8,128)(2,1)S(1)}, u32[]{:S(2)}, u32[]{:S(2)}) collective-permute-start(bf16[1568,128]{1,0:T(8,128)(2,1)S(1)} %collective-permute-done.side_ref), channel_id=1, source_target_pairs={{0,8},{8,0},{16,24},{24,16},{32,40},{40,32},{48,56},{56,48},{64,72... | collective-permute-start | bytes 1204232 | tf_op jit(solution)/shard_map/ppermute | solution.py:235

commit v7 on v6

--- a/solution.py
+++ b/solution.py
@@ -27,15 +27,17 @@
 def totals_kernel(dipole_hbm, polar_hbm, own_ref, dipole_ref, polar_ref, sem):
     components, molecules, length = dipole_ref.shape
     blocks = molecules // BLK
+    pairs = ((dipole_hbm, dipole_ref), (polar_hbm, polar_ref))
     copies = [
-        pltpu.make_async_copy(dipole_hbm, dipole_ref, sem.at[0]),
-        pltpu.make_async_copy(polar_hbm, polar_ref, sem.at[1]),
+        pltpu.make_async_copy(source.at[c], ref.at[c], sem.at[number * components + c])
+        for number, (source, ref) in enumerate(pairs)
+        for c in range(components)
     ]
     for copy in copies:
         copy.start()
-    for number, (copy, ref) in enumerate(zip(copies, (dipole_ref, polar_ref))):
-        copy.wait()
+    for number, (source, ref) in enumerate(pairs):
         for c in range(components):
+            copies[number * components + c].wait()
             at = (number * components + c) * blocks
             own_ref[at : at + blocks, :] = pair_sums(ref[c])
 
@@ -242,7 +244,7 @@
         scratch_shapes=[
             pltpu.VMEM((components, molecules, length), bf16),
             pltpu.VMEM((components, molecules, length), bf16),
-            pltpu.SemaphoreType.DMA((2,)),
+            pltpu.SemaphoreType.DMA((2 * components,)),
         ],
         compiler_params=TOTALS_PARAMS,
         cost_estimate=pl.CostEstimate(flops=4 * 32 * 64 * 3072, bytes_accessed=1200000, transcendentals=0),

time: 43.4 us -> 43.8 us (level)
  no operation moved by 1% of the time
where the time goes in v7:
time: 43.8 us; the launch traced here: 43.5 us
  blocking collectives  18.8 us (43%)
  starting transfers between devices  14.5 us (33%)
  Pallas kernels  4.67 us (11%)
  waiting for transfers between devices  4.23 us (10%)
  local copies, waits for them, and re-layouts  0.65 us (1%)
  other arithmetic  0.59 us (1%)
    all_to_all x1, blocking collectives, per_device(): shares = lax.all_to_all(sums, 'tm', 0, 0)  16.7 us
    ppermute x3, starting transfers between devices, moved(): return lax.ppermute(value, 'space', pairs)  12.6 us
    ppermute x3, waiting for transfers between devices, moved(): return lax.ppermute(value, 'space', pairs)  4.22 us
    all_gather x1, blocking collectives, per_device(): both = lax.all_gather(pack, 'space', axis_index_groups=pairs, tiled=True)  2.08 us
    ppermute x1, starting transfers between devices, per_device(): lax.ppermute(own_later, 'tm', [(i, i - 1) for i in range(1, time_size)])  1.92 us
    pallas_call x1, Pallas kernels, per_device(): pl.pallas_call(functools.partial(sums_kernel, length * time_size), out_sh...  1.92 us
    pallas_call x1, Pallas kernels, per_device(): pl.pallas_call(totals_kernel, out_shape=jax.ShapeDtypeStruct((2 * rows, l...  1.83 us
  transfers between devices with their start and end apart: 4, of which 1 were waited for; matrix products, arithmetic and copies ran while one was open for 0% of the time, Pallas kernels for 2%

profile of v7, /device:TPU:64, one launch (start us, length us, event | category | flops | bytes accessed | tf_op | source)
XLA Modules:
  0.0 43.5 jit_solution(4040132008644607375)
XLA Ops:
  0.0 0.0 copy-start
  0.0 1.8 %totals.1.own_ref = bf16[192,1024]{1,0:T(8,128)(2,1)S(1)} custom-call(bf16[3,64,1024]{2,1,0:T(8,128)(2,1)} %bitcast.12, bf16[3,64,1024]{2,1,0:T(8,128)(2,1)} %bitcast.13), custom_call_target="tpu_custom_call" | custom-call | flops 25165824 | bytes 1200000 | tf_op jit(solution)/shard_map/totals/pallas_call | solution.py:239
  1.8 0.0 copy-start.1
  1.9 0.0 copy-done
  1.9 0.6 %copy-done.1 = s32[1,64]{1,0:T(1,128)S(1)} copy-done((s32[1,64]{1,0:T(1,128)S(1)}, s32[1,64]{1,0:T(1,128)}, u32[]{:S(2)}) %copy-start.1) | copy-done | bytes 280
  2.5 0.1 pack.1.pack_ref
  2.6 2.1 %all_gather.3.both_ref.unused_ref = bf16[1568,128]{1,0:T(8,128)(2,1)S(1)} all-gather(bf16[784,128]{1,0:T(8,128)(2,1)S(1)} %pack.1.pack_ref), channel_id=1, replica_groups={{0,8},{16,24},{32,40},{48,56},{64,72},{80,88},{96,104},{112,120},{128,1..., dimensions={0}, use_global_device_ids=true | all-gather | bytes 602112 | tf_op jit(solution)/shard_map/all_gather | solution.py:270
  4.7 7.3 %collective-permute-start = (bf16[1568,128]{1,0:T(8,128)(2,1)S(1)}, bf16[1568,128]{1,0:T(8,128)(2,1)S(1)}, u32[]{:S(2)}, u32[]{:S(2)}) collective-permute-start(bf16[1568,128]{1,0:T(8,128)(2,1)S(1)} %all_gather.3.both_ref.unused_ref), channel_id=1, source_target_pairs={{0,504},{8,16},{16,8},{24,32},{32,24},{40,48},{48,40},{56,64},{64,... | collective-permute-start | bytes 1204232 | tf_op jit(solution)/shard_map/ppermute | solution.py:237
  12.0 1.9 %collective-permute-start.3 = (bf16[192,1024]{1,0:T(8,128)(2,1)S(1)}, bf16[192,1024]{1,0:T(8,128)(2,1)S(1)}, u32[]{:S(2)}, u32[]{:S(2)}) collective-permute-start(bf16[192,1024]{1,0:T(8,128)(2,1)S(1)} %totals.1.own_ref), channel_id=1, source_target_pairs={{1,0},{2,1},{3,2},{4,3},{5,4},{6,5},{7,6},{9,8},{10,9},{11,10},{12... | collective-permute-start | bytes 1179656 | tf_op jit(solution)/shard_map/ppermute | solution.py:273
  14.0 0.0 copy-start.2
  14.0 0.2 select.3
  14.2 3.4 %collective-permute-start.1 = (bf16[576,128]{1,0:T(8,128)(2,1)S(1)}, bf16[576,128]{1,0:T(8,128)(2,1)S(1)}, u32[]{:S(2)}, u32[]{:S(2)}) collective-permute-start(bf16[576,128]{1,0:T(8,128)(2,1)S(1)} %select.3), channel_id=1, source_target_pairs={{0,488},{8,32},{16,504},{24,48},{32,8},{40,64},{48,24},{56,80},{64... | collective-permute-start | bytes 442376 | tf_op jit(solution)/shard_map/ppermute | solution.py:237
  17.6 0.0 collective-permute-done.side_ref
  17.6 1.9 %collective-permute-start.2 = (bf16[1568,128]{1,0:T(8,128)(2,1)S(1)}, bf16[1568,128]{1,0:T(8,128)(2,1)S(1)}, u32[]{:S(2)}, u32[]{:S(2)}) collective-permute-start(bf16[1568,128]{1,0:T(8,128)(2,1)S(1)} %collective-permute-done.side_ref), channel_id=1, source_target_pairs={{0,8},{8,0},{16,24},{24,16},{32,40},{40,32},{48,56},{56,48},{64,72... | collective-permute-start | bytes 1204232 | tf_op jit(solution)/shard_map/ppermute | solution.py:237
  19.5 0.0 copy-done.2
  19.5 0.5 %near.1.part_ref = f32[96,1024]{1,0:T(8,128)S(1)} custom-call(s32[1]{0:T(128)} %bitcast.odd_ref, s32[24,32]{1,0:T(8,128)S(1)} %bitcast.10, bf16[1568,128]{1,0:T(8,128)(2,1)S(1)} %all_gather.3.both_ref.unused_ref, bf16[1568,128]{1,0:T(8,128)(2,1)S(1)} %collective-permute-done.side_ref), custom_call_target="tpu_custom_call" | custom-call | flops 10000000000 | bytes 1000000 | tf_op jit(solution)/shard_map/near/pallas_call | solution.py:288
  20.1 4.2 %collective-permute-done.1.far_ref = bf16[576,128]{1,0:T(8,128)(2,1)S(1)} collective-permute-done((bf16[576,128]{1,0:T(8,128)(2,1)S(1)}, bf16[576,128]{1,0:T(8,128)(2,1)S(1)}, u32[]{:S(2)}, u32[]{:S(2)}) %collective-permute-start.1) | collective-permute-done | bytes 147488 | tf_op jit(solution)/shard_map/ppermute | solution.py:237
  24.3 0.0 collective-permute-done.3.next_ref
  24.3 0.0 collective-permute-done.2.swap_ref
  24.3 1.9 %sums.1 = f32[8,4,128]{2,1,0:T(4,128)S(1)} custom-call(s32[1]{0:T(128)} %bitcast.odd_ref, s32[24,32]{1,0:T(8,128)S(1)} %bitcast.11, f32[96,1024]{1,0:T(8,128)S(1)} %near.1.part_ref, bf16[576,128]{1,0:T(8,128)(2,1)S(1)} %collective-permute-done.1.far_ref, bf16[1568,128]{1,0:T(8,128)(2,1)S(1)} %collective-permute-done.2.swap_ref, ...), custom_call_target="tpu_custom_call" | custom-call | flops 600000000 | bytes 2500000 | tf_op jit(solution)/shard_map/sums/pallas_call | solution.py:297
  26.2 16.7 %all_to_all.5 = f32[8,4,128]{2,1,0:T(4,128)S(1)} all-to-all(f32[8,4,128]{2,1,0:T(4,128)S(1)} %sums.1), channel_id=1, replica_groups=mesh['space'=64,'tm'=8] {'tm'}, dimensions={0} | all-to-all | bytes 32768 | tf_op jit(solution)/shard_map/all_to_all | solution.py:308
  42.9 0.6 %reduce_sum.9 = f32[4,128]{1,0:T(4,128)} reduce(f32[8,4,128]{2,1,0:T(4,128)S(1)} %all_to_all.5, f32[]{:T(128)} %constant.20.clone.1), dimensions={0}, to_apply=%region_0.1 | reduce | flops 3584 | bytes 18436 | tf_op jit(solution)/shard_map/reduce_sum | solution.py:309
Async XLA Ops:
  0.0 1.9 %copy-start = (s32[1,64,24]{1,2,0:T(8,128)S(1)}, s32[1,64,24]{1,2,0:T(8,128)}, u32[]{:S(2)}) copy-start(s32[1,64,24]{1,2,0:T(8,128)} %param.8) | copy-start | bytes 18436
  1.8 0.7 %copy-start.1 = (s32[1,64]{1,0:T(1,128)S(1)}, s32[1,64]{1,0:T(1,128)}, u32[]{:S(2)}) copy-start(s32[1,64]{1,0:T(1,128)} %counts_ref.1) | copy-start | bytes 772
  4.7 12.9 %collective-permute-start = (bf16[1568,128]{1,0:T(8,128)(2,1)S(1)}, bf16[1568,128]{1,0:T(8,128)(2,1)S(1)}, u32[]{:S(2)}, u32[]{:S(2)}) collective-permute-start(bf16[1568,128]{1,0:T(8,128)(2,1)S(1)} %all_gather.3.both_ref.unused_ref), channel_id=1, source_target_pairs={{0,504},{8,16},{16,8},{24,32},{32,24},{40,48},{48,40},{56,64},{64,... | collective-permute-start | bytes 1204232 | tf_op jit(solution)/shard_map/ppermute | solution.py:237
  12.0 12.3 %collective-permute-start.3 = (bf16[192,1024]{1,0:T(8,128)(2,1)S(1)}, bf16[192,1024]{1,0:T(8,128)(2,1)S(1)}, u32[]{:S(2)}, u32[]{:S(2)}) collective-permute-start(bf16[192,1024]{1,0:T(8,128)(2,1)S(1)} %totals.1.own_ref), channel_id=1, source_target_pairs={{1,0},{2,1},{3,2},{4,3},{5,4},{6,5},{7,6},{9,8},{10,9},{11,10},{12... | collective-permute-start | bytes 1179656 | tf_op jit(solution)/shard_map/ppermute | solution.py:273
  14.0 5.6 %copy-start.2 = (s32[32,24]{0,1:T(8,128)S(1)}, s32[32,24]{0,1:T(8,128)}, u32[]{:S(2)}) copy-start(s32[32,24]{0,1:T(8,128)} %param.9) | copy-start | bytes 9220
  14.2 10.1 %collective-permute-start.1 = (bf16[576,128]{1,0:T(8,128)(2,1)S(1)}, bf16[576,128]{1,0:T(8,128)(2,1)S(1)}, u32[]{:S(2)}, u32[]{:S(2)}) collective-permute-start(bf16[576,128]{1,0:T(8,128)(2,1)S(1)} %select.3), channel_id=1, source_target_pairs={{0,488},{8,32},{16,504},{24,48},{32,8},{40,64},{48,24},{56,80},{64... | collective-permute-start | bytes 442376 | tf_op jit(solution)/shard_map/ppermute | solution.py:237
  17.6 6.7 %collective-permute-start.2 = (bf16[1568,128]{1,0:T(8,128)(2,1)S(1)}, bf16[1568,128]{1,0:T(8,128)(2,1)S(1)}, u32[]{:S(2)}, u32[]{:S(2)}) collective-permute-start(bf16[1568,128]{1,0:T(8,128)(2,1)S(1)} %collective-permute-done.side_ref), channel_id=1, source_target_pairs={{0,8},{8,0},{16,24},{24,16},{32,40},{40,32},{48,56},{56,48},{64,72... | collective-permute-start | bytes 1204232 | tf_op jit(solution)/shard_map/ppermute | solution.py:237
